TPU v7x, 128 devices: a whole 4x4x4 slice. The times are simulated.
128 devices in a mesh: section: 4 (over x), expert: 16 (over y, z_lo, core), dp: 2 (over z_hi).
Axes of the slice: x: 4, y: 4, z: 4 (z_hi: 2, z_lo: 2; z = z_hi * 2 + z_lo), core: 2. Of those that a mesh axis runs over, the one named last changes fastest.
Arguments:
- tokens: bfloat16 [4, 2, 2048, 3584], P('section', 'dp', 'expert'), may hold values from -6 to 6
- grad_out: bfloat16 [4, 2, 2048, 3584], P('section', 'dp', 'expert'), may hold values from -6 to 6
- expert_ids: int32 [4, 2, 2048, 2], P('section', 'dp', 'expert'), may hold values from 0 to 15, all different within a row; in each aligned block of 128 rows (0 to 127, 128 to 255, ..., all dimensions but the last counted through in order) at most 24 rows name the same one
- route_weight: float32 [4, 2, 2048, 2], P('section', 'dp', 'expert'), may hold values from 0.1 to 1
- w_gate: bfloat16 [4, 16, 3584, 1024], P('section', 'expert', None, 'dp'), may hold values from -0.09375 to 0.09375
- w_up: bfloat16 [4, 16, 3584, 1024], P('section', 'expert', None, 'dp'), may hold values from -0.09375 to 0.09375
- w_down: bfloat16 [4, 16, 1024, 3584], P('section', 'expert', 'dp'), may hold values from -0.1875 to 0.1875
Outputs:
- next_input: bfloat16 [4, 2, 2048, 3584], P('section', 'dp', 'expert')
- prev_grad: bfloat16 [4, 2, 2048, 3584], P('section', 'dp', 'expert')
- grad_gate: bfloat16 [4, 16, 3584, 1024], P('section', 'expert', None, 'dp')
- grad_up: bfloat16 [4, 16, 3584, 1024], P('section', 'expert', None, 'dp')
- grad_down: bfloat16 [4, 16, 1024, 3584], P('section', 'expert', 'dp')
Inputs may be any that keep to these rules, and one draw needn't show every extreme that they name: `expert_ids`: each row names 2 different experts; within each aligned block of 128 rows (the rows of one device) no expert is named more than 24 times, a bound that some block reaches.
All inputs are finite; a program needn't handle non-finite values.
Results may differ from a plain program's by a relative error of at most 0.0065.
Values may be sent and summed in bfloat16 or wider, within the bound.
No kernel may reach another device: no remote copies, remote signals or barrier semaphores. Data moves between devices by JAX's collectives and lax.ppermute only.
A program may use at most 192 MiB of HBM per device.

v0:
```python
import jax
import jax.numpy as jnp
from jax import lax
from jax.experimental import pallas as pl
from jax.experimental.pallas import tpu as pltpu
from jax.sharding import PartitionSpec as P

GROUP = ("expert", "dp")
BF = jnp.bfloat16
F32 = jnp.float32


def place(y, z, c):
    return (((y * 2 + z % 2) * 2 + c) * 2) + z // 2


def shifted(x, dy, dz, dc):
    pairs = [
        (place(y, z, c), place((y + dy) % 4, (z + dz) % 4, c ^ dc))
        for y in range(4)
        for z in range(4)
        for c in range(2)
    ]
    return lax.ppermute(x, GROUP, pairs)


def shift_y(x, by):
    return x if by % 4 == 0 else shifted(x, by, 0, 0)


def shift_z(x, by):
    return x if by % 4 == 0 else shifted(x, 0, by, 0)


def swap_core(x):
    return shifted(x, 0, 0, 1)


def after(x, done):
    return lax.optimization_barrier((x, done))[0]


def from_behind(x, axis, by):
    count = lax.axis_size(axis)
    pairs = [(i, i + by) for i in range(count) if 0 <= i + by < count]
    return lax.ppermute(x, axis, pairs)


def slot_codes(ids, experts, slot_rows):
    rows = ids.shape[-2]
    onehot = (ids[..., None] == jnp.arange(experts, dtype=F32)).astype(F32)
    named = jnp.sum(onehot, axis=-2).astype(BF)
    before = jnp.tri(rows, k=-1, dtype=BF)
    earlier = jnp.einsum("ij,...je->...ie", before, named, preferred_element_type=F32)
    position = jnp.sum(onehot * earlier[..., None, :], axis=-1)
    return (ids * slot_rows + position).astype(jnp.int32)


def chosen(codes, weights, targets):
    hits = [codes[..., k, None] == targets for k in range(codes.shape[-1])]
    weight = sum(jnp.sum(jnp.where(h, weights[..., k, None], 0.0), axis=-2) for k, h in enumerate(hits))
    return [h.astype(BF) for h in hits], hits[0].astype(BF) + hits[1].astype(BF), weight


def in_three(w):
    high = lax.reduce_precision(w, 8, 7)
    middle = lax.reduce_precision(w - high, 8, 7)
    return high, middle, w - high - middle


def mm(a, b):
    return jnp.dot(a, b, preferred_element_type=F32)


def mm_last(a, b):
    return lax.dot_general(a, b, (((1,), (1,)), ((), ())), preferred_element_type=F32)


def mm_first(a, b):
    return lax.dot_general(a, b, (((0,), (0,)), ((), ())), preferred_element_type=F32)


def kernel_call(body, grid, in_specs, out_specs, out_shape, scratch=()):
    return pl.pallas_call(
        body,
        grid=(grid,),
        in_specs=in_specs,
        out_specs=out_specs,
        out_shape=out_shape,
        scratch_shapes=scratch,
        compiler_params=pltpu.CompilerParams(vmem_limit_bytes=40 * 1024 * 1024),
        cost_estimate=pl.CostEstimate(flops=1, bytes_accessed=1, transcendentals=0),
    )


def whole(x):
    return pl.BlockSpec(x.shape, lambda i: (0, 0))


def columns(rows, n):
    return pl.BlockSpec((rows, n), lambda i: (0, i))


def rows_block(n, width):
    return pl.BlockSpec((n, width), lambda i: (i, 0))


def forward(pieces, gate_matrix, up_matrix):
    count, rows = len(pieces), pieces[0].shape[0]
    depth, units = gate_matrix.shape
    n = units // 2

    def body(*refs):
        gate, up, outs = refs[count], refs[count + 1], refs[count + 2 :]
        for i in range(count):
            x = refs[i][...]
            g, u = mm(x, gate[...]), mm(x, up[...])
            outs[3 * i][...] = g
            outs[3 * i + 1][...] = u
            outs[3 * i + 2][...] = (g * jax.nn.sigmoid(g) * u).astype(BF)

    shapes = [jax.ShapeDtypeStruct((rows, units), t) for t in (F32, F32, BF)] * count
    outs = kernel_call(
        body,
        2,
        [whole(x) for x in pieces] + [columns(depth, n)] * 2,
        [columns(rows, n)] * (3 * count),
        shapes,
    )(*pieces, gate_matrix, up_matrix)
    return [outs[3 * i : 3 * i + 3] for i in range(count)]


def outputs(hidden, down_matrix):
    count, rows = len(hidden), hidden[0].shape[0]
    units, width = down_matrix.shape
    n = width // 7

    def body(*refs):
        for i in range(count):
            refs[count + 1 + i][...] = mm(refs[i][...], refs[count][...]).astype(BF)

    return kernel_call(
        body,
        7,
        [whole(h) for h in hidden] + [columns(units, n)],
        [columns(rows, n)] * count,
        [jax.ShapeDtypeStruct((rows, width), BF)] * count,
    )(*hidden, down_matrix)


def hidden_grads(pieces, down_matrix):
    count, rows = len(pieces), pieces[0].shape[0]
    units, width = down_matrix.shape
    n = units // 2

    def body(*refs):
        for i in range(count):
            refs[count + 1 + i][...] = mm_last(refs[i][...], refs[count][...])

    return kernel_call(
        body,
        2,
        [whole(g) for g in pieces] + [rows_block(n, width)],
        [columns(rows, n)] * count,
        [jax.ShapeDtypeStruct((rows, units), F32)] * count,
    )(*pieces, down_matrix)


def backward(groups, slot, gate_pre, up_pre, hidden_grad, gate_matrix, up_matrix):
    used_s = sorted({s for _, those in groups for s in those})
    pairs = sorted((s, t) for t, those in groups for s in those)
    rows, units = gate_pre[used_s[0]].shape
    width = gate_matrix.shape[0]
    n = width // 7
    counts = [2 * len(those) * slot for _, those in groups]
    starts = [sum(counts[:i]) for i in range(len(groups))]
    total = sum(counts)
    many, those_s = len(groups), len(used_s)

    def body(*refs):
        gates = dict(zip(used_s, refs[:those_s]))
        ups = dict(zip(used_s, refs[those_s : 2 * those_s]))
        refs = refs[2 * those_s :]
        grads, (gate, up), refs = refs[:many], refs[many : many + 2], refs[many + 2 :]
        backs, (gate_out, up_out, gate_rows, up_rows) = refs[:many], refs[many:]

        @pl.when(pl.program_id(0) == 0)
        def _():
            for i, (t, those) in enumerate(groups):
                terms = {}
                for d in range(2):
                    for s in those:
                        here = pl.ds((t * 2 + d) * slot, slot)
                        g, u = gates[s][here, :], ups[s][here, :]
                        h = grads[i][pl.ds((d * 4 + s) * slot, slot), :]
                        sig = jax.nn.sigmoid(g)
                        terms[d, s] = (h * u * sig * (1.0 + g * (1.0 - sig)), h * g * sig)
                order = [terms[d, s] for d in range(2) for s in those]
                for which, by_t, by_s in ((0, gate_rows, gate_out), (1, up_rows, up_out)):
                    for k in range(0, len(order), 2):
                        pair = jnp.concatenate([order[k][which], order[k + 1][which]], axis=0)
                        by_t[pl.ds(starts[i] + k * slot, 2 * slot), :] = pair.astype(BF)
                    for s in those:
                        pair = jnp.concatenate([terms[0, s][which], terms[1, s][which]], axis=0)
                        by_s[pl.ds(pairs.index((s, t)) * 2 * slot, 2 * slot), :] = pair.astype(BF)

        back = mm_last(gate_rows[...], gate[...]) + mm_last(up_rows[...], up[...])
        for i in range(many):
            backs[i][...] = back[starts[i] : starts[i] + counts[i]].astype(BF)

    both = jax.ShapeDtypeStruct((total, units), BF)
    operands = [gate_pre[s] for s in used_s] + [up_pre[s] for s in used_s]
    operands += [hidden_grad[t] for t, _ in groups]
    outs = kernel_call(
        body,
        7,
        [whole(a) for a in operands] + [rows_block(n, units)] * 2,
        [columns(count, n) for count in counts] + [whole(both)] * 2,
        [jax.ShapeDtypeStruct((count, width), BF) for count in counts] + [both] * 2,
        [pltpu.VMEM(both.shape, BF)] * 2,
    )(*operands, gate_matrix, up_matrix)
    grads = [
        {pair: a[k * 2 * slot : (k + 1) * 2 * slot] for k, pair in enumerate(pairs)} for a in outs[many:]
    ]
    return outs[:many], grads[0], grads[1]


def local(tokens, grad_out, expert_ids, route_weight, w_gate, w_up, w_down):
    inputs = tokens[0, 0]
    upstream = grad_out[0, 0]
    weights = route_weight[0, 0]
    gate_matrix, up_matrix, down_matrix = w_gate[0, 0], w_up[0, 0], w_down[0, 0]
    experts = lax.axis_size("expert")
    rows, per_token = weights.shape
    width = inputs.shape[1]
    split = rows // 2
    slot = 3 * rows * per_token // (2 * experts)
    flat = 8 * slot
    me = lax.axis_index("expert")
    y, zl, c = me // 4, (me // 2) % 2, me % 2

    ids = expert_ids[0, 0].astype(F32)
    fields = [ids] + [jnp.stack([a[:, k] for a in in_three(weights)], axis=1) for k in range(per_token)]
    fields = jnp.concatenate(fields, axis=1).astype(BF)
    codes = slot_codes(ids, experts, slot)
    step = jnp.arange(4, dtype=jnp.int32)
    two = jnp.arange(2, dtype=jnp.int32)
    slots = jnp.arange(slot, dtype=jnp.int32)
    dest_y = ((y + step) % 4) * 4
    targets_z = (
        (dest_y[None, :, None] + zl * 2 + (c ^ two)[:, None, None]) * slot + slots
    ).reshape(-1)
    targets_y = (
        (
            dest_y[None, :, None, None]
            + (zl ^ two)[None, None, :, None] * 2
            + (c ^ two)[:, None, None, None]
        )
        * slot
        + slots
    ).reshape(-1)
    each_y, pick_y, _ = chosen(codes, weights, targets_y)
    own, sib = [
        mm_first(pick_y[:, dc * flat : (dc + 1) * flat], inputs).astype(BF) for dc in range(2)
    ]
    message = jnp.concatenate(
        [after(upstream, sib), jnp.pad(fields.T, ((0, 0), (0, width - rows)))], axis=0
    )
    near1, near3 = shift_z(message, 1), shift_z(message, 3)
    sib = swap_core(sib)
    along_y = [
        jnp.concatenate([a[t * 2 * slot : (t + 1) * 2 * slot] for a in (own, sib)]) for t in range(4)
    ]
    y1, y3 = shift_y(along_y[1], 1), shift_y(along_y[3], 3)

    near1, near3, y1, y3, far_y = lax.optimization_barrier((near1, near3, y1, y3, along_y[2]))
    y2 = shift_y(far_y, 2)
    far_a, far_b = shift_z(near1[:split], 1), shift_z(near3[split:], 3)
    ring_tables = [fields, near1[rows:, :rows].T, far_b[rows - split :, :rows].T, near3[rows:, :rows].T]

    def picks(table):
        table = table.astype(F32)
        parts = [table[:, per_token + 3 * k : per_token + 3 * k + 3] for k in range(per_token)]
        weigh = jnp.stack([p[:, 0] + p[:, 1] + p[:, 2] for p in parts], axis=-1)
        return chosen(slot_codes(table[:, :per_token], experts, slot), weigh, targets_z)[1:]

    pick_z, slot_weight_z = zip(*[picks(a) for a in ring_tables])
    far_a, far_b, near1, near3, late_upstream = lax.optimization_barrier(
        (far_a, far_b, near1, near3, upstream)
    )
    far = jnp.concatenate([far_a, far_b[: rows - split]])
    sel = [
        (slot_weight_z[s][:, None] * mm_first(pick_z[s], block)).astype(BF).reshape(2, 4, slot, width)
        for s, block in enumerate((late_upstream, near1[:rows], far, near3[:rows]))
    ]
    cross = [jnp.stack([a[1, t] for t in those for a in sel]) for those in ((1, 3), (0, 2))]

    sel, cross, y1, y2, y3 = lax.optimization_barrier((sel, cross, y1, y2, y3))
    by_y = [along_y[0], y1, y2, y3]
    same, other = [
        jnp.concatenate([a[k * slot : (k + 1) * slot] for a in by_y for k in (dl, 2 + dl)])
        for dl in range(2)
    ]
    x1, x3 = shift_z(other, 1), shift_z(other, 3)
    odd, even = swap_core(cross[0]), swap_core(cross[1])
    sib = [even[:4], odd[:4], even[4:], odd[4:]]
    out_y = [
        jnp.concatenate([jnp.stack([sel[s][0, t] for s in range(4)]), sib[t]]).reshape(flat, width)
        for t in range(4)
    ]
    g1, g3 = shift_y(out_y[1], 1), shift_y(out_y[3], 3)

    x1, x3, g1, g3, same_far, out_far = lax.optimization_barrier((x1, x3, g1, g3, same, out_y[2]))
    x2, g2 = shift_z(same_far, 2), shift_y(out_far, 2)
    ahead = forward([x1, x3, same_far], gate_matrix, up_matrix)
    out1, out3 = outputs([ahead[0][2], ahead[1][2]], down_matrix)
    grad1, grad3, grad0 = hidden_grads([g1, g3, out_y[0]], down_matrix)
    gate_pre, up_pre, hidden = [{0: ahead[2][i], 1: ahead[0][i], 3: ahead[1][i]} for i in range(3)]
    early = ((1, (0, 1, 3)), (3, (0, 1, 3)))
    (back1, back3), gate_grad, up_grad = backward(
        early, slot, gate_pre, up_pre, {1: grad1, 3: grad3}, gate_matrix, up_matrix
    )

    x2, g2, out1, out3, back1, back3 = lax.optimization_barrier((x2, g2, out1, out3, back1, back3))
    e1, e3 = shift_z(out1, -1), shift_z(out3, -3)
    b1, b3 = shift_y(back1, -1), shift_y(back3, -3)
    ((gate_pre[2], up_pre[2], hidden[2]),) = forward([x2], gate_matrix, up_matrix)
    (grad2,) = hidden_grads([g2], down_matrix)
    out2, out0 = outputs([hidden[2], hidden[0]], down_matrix)
    rest = ((0, (0, 1, 2, 3)), (2, (0, 1, 2, 3)), (1, (2,)), (3, (2,)))
    (back0, back2, back1, back3), more_gate, more_up = backward(
        rest,
        slot,
        gate_pre,
        up_pre,
        {0: grad0, 1: grad1, 2: grad2, 3: grad3},
        gate_matrix,
        up_matrix,
    )
    gate_grad, up_grad = {**gate_grad, **more_gate}, {**up_grad, **more_up}

    e1, e3, b1, b3, out0, out2, back0, back1, back2, back3 = lax.optimization_barrier(
        (e1, e3, b1, b3, out0, out2, back0, back1, back2, back3)
    )
    e2, b2 = shift_z(out2, -2), shift_y(back2, -2)
    far1, far3 = shift_y(back1, -1), shift_y(back3, -3)
    swapped = swap_core(back0[4 * slot :])
    back0 = back0.reshape(2, 4, slot, width)
    b1, b3 = [a.reshape(2, 3, slot, width) for a in (b1, b3)]
    late_g, late_hidden, _ = lax.optimization_barrier(((out_y[0], g1, g2, g3), hidden, e1))
    late_hidden = jnp.stack([late_hidden[s].reshape(4, 2, slot, -1) for s in range(4)], axis=2)
    down_total = mm_first(late_hidden.reshape(4 * flat, -1), jnp.concatenate(late_g)).astype(BF)

    e1, e2, e3, b2, far1, far3, swapped = lax.optimization_barrier(
        (e1, e2, e3, b2, far1, far3, swapped)
    )
    swapped = swapped.reshape(4, slot, width)
    b2 = b2.reshape(2, 4, slot, width)
    far1, far3 = [a.reshape(2, 1, slot, width) for a in (far1, far3)]
    others = swap_core(jnp.concatenate([b2[1], b1[1], b3[1], far1[1], far3[1]]))

    def in_order(whole0, part1, whole2, part3, rest1, rest3):
        part1, part3 = [[p[0], p[1], r[0], p[2]] for p, r in ((part1, rest1), (part3, rest3))]
        return [whole0, part1, whole2, part3]

    back = [
        in_order(back0[0], b1[0], b2[0], b3[0], far1[0], far3[0]),
        in_order(swapped, others[4:7], others[:4], others[7:10], others[10:11], others[11:]),
    ]

    def by_token(s):
        rows_of = jnp.stack([back[dc][t][s] for dc in range(2) for t in range(4)])
        return mm(pick_z[s], rows_of.reshape(-1, width))

    both = [
        (out0.astype(F32) + e2.astype(F32)).astype(BF).reshape(4, 2, slot, width),
        (e1.astype(F32) + e3.astype(F32)).astype(BF).reshape(4, 2, slot, width),
    ]
    both = [jnp.stack([a[t] for a in both]) for t in range(4)]
    m1, m3 = shift_y(both[1], -1), shift_y(both[3], -3)
    far = by_token(2).astype(BF)
    far_a, far_b = shift_z(far[:split], 1), shift_z(far[split:], -1)
    up_z, down_z, here = by_token(3), by_token(1), by_token(0)

    far_a, far_b, m1, m3, both_far = lax.optimization_barrier((far_a, far_b, m1, m3, both[2]))
    up_z = jnp.concatenate([up_z[:split] + far_a.astype(F32), up_z[split:]]).astype(BF)
    down_z = jnp.concatenate([down_z[:split], down_z[split:] + far_b.astype(F32)]).astype(BF)
    from_down, from_up = shift_z(up_z, 1), shift_z(down_z, -1)
    m2 = shift_y(both_far, -2)
    swapped = swap_core(jnp.stack([both[0][:, 1], m1[:, 1], m3[:, 1]]))
    late_x, late_gate, _ = lax.optimization_barrier(((same, x1, x2, x3), gate_grad, far_a))

    def by_s(grads):
        return jnp.concatenate([grads[s, t] for s in range(4) for t in range(4)])

    late_x = jnp.concatenate(late_x)
    gate_total = mm_first(late_x, by_s(late_gate)).astype(BF)

    sib = [swapped[0], swapped[1], swap_core(m2[:, 1]), swapped[2]]
    back = jnp.stack([both[0][:, 0], m1[:, 0], m2[:, 0], m3[:, 0]] + sib).reshape(-1, width)
    mixed = sum(weights[:, k, None] * mm(each_y[k], back) for k in range(per_token)).astype(BF)
    next_input = from_behind(mixed, "section", 1)
    input_grad = (here + from_down.astype(F32) + from_up.astype(F32)).astype(BF)
    prev_grad = from_behind(input_grad, "section", -1)
    late_x, late_up, _ = lax.optimization_barrier((late_x, up_grad, m2))
    up_total = mm_first(late_x, by_s(late_up)).astype(BF)
    return (
        next_input[None, None],
        prev_grad[None, None],
        gate_total[None, None],
        up_total[None, None],
        down_total[None, None],
    )


def solution(mesh):
    return jax.shard_map(
        local,
        mesh=mesh,
        in_specs=(
            P("section", "dp", "expert", None),
            P("section", "dp", "expert", None),
            P("section", "dp", "expert", None),
            P("section", "dp", "expert", None),
            P("section", "expert", None, "dp"),
            P("section", "expert", None, "dp"),
            P("section", "expert", "dp", None),
        ),
        out_specs=(
            P("section", "dp", "expert", None),
            P("section", "dp", "expert", None),
            P("section", "expert", None, "dp"),
            P("section", "expert", None, "dp"),
            P("section", "expert", "dp", None),
        ),
        check_vma=False,
    )
```

profile of v0, /device:TPU:6, one launch (start us, length us, event | category | flops | bytes accessed | tf_op | source)
XLA Modules:
  0.0 286.5 jit_solution(11527872026369149370)
XLA Ops:
  17.0 15.4 %collective-permute-done.1 = bf16[136,3584]{1,0:T(8,128)(2,1)} collective-permute-done((bf16[136,3584]{1,0:T(8,128)(2,1)}, bf16[136,3584]{1,0:T(8,128)(2,1)}, u32[]{:S(2)}, u32[]{:S(2)}) %collective-permute-start.1) | collective-permute-done | bytes 974880 | tf_op jit(solution)/shard_map/ppermute | solution.py:24
  34.2 3.0 %collective-permute-start.6 = (bf16[72,3584]{1,0:T(8,128)(2,1)S(1)}, bf16[72,3584]{1,0:T(8,128)(2,1)S(1)}, u32[]{:S(2)}, u32[]{:S(2)}) collective-permute-start(bf16[72,3584]{1,0:T(8,128)(2,1)S(1)} %slice.821), channel_id=1, source_target_pairs={{0,5},{2,7},{4,0},{6,2},{1,4},{3,6},{5,1},{7,3},{8,13},{10,15},{12... | collective-permute-start | bytes 1548296 | tf_op jit(solution)/shard_map/ppermute | solution.py:24
  39.6 3.3 %collective-permute-start.7 = (bf16[96,3584]{1,0:T(8,128)(2,1)S(1)}, bf16[96,3584]{1,0:T(8,128)(2,1)S(1)}, u32[]{:S(2)}, u32[]{:S(2)}) collective-permute-start(bf16[96,3584]{1,0:T(8,128)(2,1)S(1)} %pad_maximum_fusion.6), channel_id=1, source_target_pairs={{0,16},{2,18},{4,20},{6,22},{1,17},{3,19},{5,21},{7,23},{8,24},{10... | collective-permute-start | bytes 2064392 | tf_op jit(solution)/shard_map/ppermute | solution.py:24
  42.9 5.2 %collective-permute-done.6 = bf16[72,3584]{1,0:T(8,128)(2,1)S(1)} collective-permute-done((bf16[72,3584]{1,0:T(8,128)(2,1)S(1)}, bf16[72,3584]{1,0:T(8,128)(2,1)S(1)}, u32[]{:S(2)}, u32[]{:S(2)}) %collective-permute-start.6) | collective-permute-done | bytes 516128 | tf_op jit(solution)/shard_map/ppermute | solution.py:24
  48.4 4.3 %collective-permute-done.5 = bf16[64,3584]{1,0:T(8,128)(2,1)S(1)} collective-permute-done((bf16[64,3584]{1,0:T(8,128)(2,1)S(1)}, bf16[64,3584]{1,0:T(8,128)(2,1)S(1)}, u32[]{:S(2)}, u32[]{:S(2)}) %collective-permute-start.5) | collective-permute-done | bytes 458784 | tf_op jit(solution)/shard_map/ppermute | solution.py:24
  58.5 3.2 %collective-permute-start.9 = (bf16[192,3584]{1,0:T(8,128)(2,1)S(1)}, bf16[192,3584]{1,0:T(8,128)(2,1)S(1)}, u32[]{:S(2)}, u32[]{:S(2)}) collective-permute-start(bf16[192,3584]{1,0:T(8,128)(2,1)S(1)} %get-tuple-element.356), channel_id=1, source_target_pairs={{0,5},{2,7},{4,0},{6,2},{1,4},{3,6},{5,1},{7,3},{8,13},{10,15},{12... | collective-permute-start | bytes 4128776 | tf_op jit(solution)/shard_map/ppermute | solution.py:24
  71.9 18.4 %collective-permute-done.8.refs_0_ = bf16[192,3584]{1,0:T(8,128)(2,1)S(1)} collective-permute-done((bf16[192,3584]{1,0:T(8,128)(2,1)S(1)}, bf16[192,3584]{1,0:T(8,128)(2,1)S(1)}, u32[]{:S(2)}, u32[]{:S(2)}) %collective-permute-start.8) | collective-permute-done | bytes 1376288 | tf_op jit(solution)/shard_map/ppermute | solution.py:24
  90.4 10.9 %collective-permute-done.11.refs_0_ = bf16[192,3584]{1,0:T(8,128)(2,1)S(1)} collective-permute-done((bf16[192,3584]{1,0:T(8,128)(2,1)S(1)}, bf16[192,3584]{1,0:T(8,128)(2,1)S(1)}, u32[]{:S(2)}, u32[]{:S(2)}) %collective-permute-start.11) | collective-permute-done | bytes 1376288 | tf_op jit(solution)/shard_map/ppermute | solution.py:24
  103.3 2.9 collective-permute-start.15
  106.2 5.4 %shard_map.110 = (f32[192,512]{1,0:T(8,128)S(1)}, f32[192,512]{1,0:T(8,128)S(1)}, bf16[192,512]{1,0:T(8,128)(2,1)S(1)}, f32[192,512]{1,0:T(8,128)S(1)}, f32[192,...) custom-call(bf16[192,3584]{1,0:T(8,128)(2,1)S(1)} %collective-permut, ...), custom_call_target="tpu_custom_call" | custom-call | flops 1 | bytes 1 | tf_op jit(solution)/shard_map/pallas_call | solution.py:123
  113.1 4.4 %shard_map.111 = (bf16[192,3584]{1,0:T(8,128)(2,1)}, bf16[192,3584]{1,0:T(8,128)(2,1)}) custom-call(bf16[192,512]{1,0:T(8,128)(2,1)S(1)} %get-tuple-element.254.refs_0_, bf16[192,512]{1,0:T(8,128)(2,1)S(1)} %get-tuple-element.256.refs_1_, bf16[512,3584]{1,0:T(8,128)(2,1)S(1)} %bitcast.308), custom_call_target="tpu_custom_call" | custom-call | flops 1 | bytes 1 | tf_op jit(solution)/shard_map/pallas_call | solution.py:142
  121.5 3.9 %shard_map.112 = (f32[192,512]{1,0:T(8,128)S(1)}, f32[192,512]{1,0:T(8,128)S(1)}, f32[192,512]{1,0:T(8,128)S(1)}) custom-call(bf16[192,3584]{1,0:T(8,128)(2,1)S(1)} %copy-done.23, bf16[192,3584]{1,0:T(8,128)(2,1)S(1)} %copy-done.26, bf16[192,3584]{1,0:T(8,128)(2,1)S(1)} %bitcast.312, bf16[512,3584]{1,0:T(8,128)(2,1)S(1)} %bitcast.309), custom_call_target="tpu_custom_call" | custom-call | flops 1 | bytes 1 | tf_op jit(solution)/shard_map/pallas_call | solution.py:160
  125.6 5.1 %shard_map.113 = (bf16[144,3584]{1,0:T(8,128)(2,1)}, bf16[144,3584]{1,0:T(8,128)(2,1)}, bf16[288,512]{1,0:T(8,128)(2,1)S(1)}, bf16[288,512]{1,0:T(8,128)(2,1)S(1)}) custom-call(f32[192,512]{1,0:T(8,128)S(1)} %copy-done.19, f32[192,512]{1,0:T(8,128)S(1)} %get-tuple-element.162.refs_1_, f32[192,512]{1,0:T(8,128)S(1)} %copy-done.15, f32[192,512]{1,0:T(8,128)S(1)} %copy-done.21, ...), custom_call_target="tpu_custom_call" | custom-call | flops 1 | bytes 1 | tf_op jit(solution)/shard_map/pallas_call | solution.py:214
  130.7 4.9 %collective-permute-done.14.refs_0_ = bf16[192,3584]{1,0:T(8,128)(2,1)} collective-permute-done((bf16[192,3584]{1,0:T(8,128)(2,1)S(1)}, bf16[192,3584]{1,0:T(8,128)(2,1)}, u32[]{:S(2)}, u32[]{:S(2)}) %collective-permute-start.14) | collective-permute-done | bytes 1376288 | tf_op jit(solution)/shard_map/ppermute | solution.py:24
  143.1 3.6 %shard_map.114 = (f32[192,512]{1,0:T(8,128)S(1)}, f32[192,512]{1,0:T(8,128)S(1)}, bf16[192,512]{1,0:T(8,128)(2,1)S(1)}) custom-call(bf16[192,3584]{1,0:T(8,128)(2,1)} %collective-permute-done.14.refs_0_, bf16[3584,512]{1,0:T(8,128)(2,1)S(1)} %bitcast.302, bf16[3584,512]{1,0:T(8,128)(2,1)S(1)} %bitcast.307), custom_call_target="tpu_custom_call" | custom-call | flops 1 | bytes 1 | tf_op jit(solution)/shard_map/pallas_call | solution.py:123
  147.4 2.9 shard_map.116.refs_9_
  150.3 3.1 %shard_map.115 = (bf16[192,3584]{1,0:T(8,128)(2,1)S(1)}, bf16[192,3584]{1,0:T(8,128)(2,1)S(1)}) custom-call(bf16[192,512]{1,0:T(8,128)(2,1)S(1)} %get-tuple-element.255.refs_0_, bf16[192,512]{1,0:T(8,128)(2,1)S(1)} %get-tuple-element.253.refs_1_, bf16[512,3584]{1,0:T(8,128)(2,1)S(1)} %bitcast.311), custom_call_target="tpu_custom_call" | custom-call | flops 1 | bytes 1 | tf_op jit(solution)/shard_map/pallas_call | solution.py:142
  153.5 7.6 %shard_map.117 = (bf16[192,3584]{1,0:T(8,128)(2,1)S(1)}, bf16[192,3584]{1,0:T(8,128)(2,1)S(1)}, bf16[48,3584]{1,0:T(8,128)(2,1)S(1)}, bf16[48,3584]{1,0:T(8,128)...) custom-call(f32[192,512]{1,0:T(8,128)S(1)} %copy-done.19, ...), custom_call_target="tpu_custom_call" | custom-call | flops 1 | bytes 1 | tf_op jit(solution)/shard_map/pallas_call | solution.py:214
  161.2 3.2 %collective-permute-done.19 = bf16[144,3584]{1,0:T(8,128)(2,1)} collective-permute-done((bf16[144,3584]{1,0:T(8,128)(2,1)}, bf16[144,3584]{1,0:T(8,128)(2,1)}, u32[]{:S(2)}, u32[]{:S(2)}) %collective-permute-start.19) | collective-permute-done | bytes 1032224 | tf_op jit(solution)/shard_map/ppermute | solution.py:24
  175.6 5.6 %fusion.9 = bf16[1,1,512,3584]{3,2,1,0:T(8,128)(2,1)} fusion(bf16[768,512]{1,0:T(8,128)(2,1)S(1)} %bitcast.353, bf16[192,3584]{1,0:T(8,128)(2,1)S(1)} %copy-done.27, bf16[192,3584]{1,0:T(8,128)(2,1)} %collective-permute-done.15.refs_0_, bf16[192,3584]{1,0:T(8,128)(2,1)S(1)} %copy-done.24, bf16[192,3584]{1,0:T(8,128)(2,1)S(1)} %bitcast.313), kind=kOutput, calls=%fused_computation.12 | convolution fusion | flops 2842427392 | bytes 9961472 | tf_op jit(solution)/shard_map/dot_general | solution.py:80
  183.4 24.2 %collective-permute-done.22 = bf16[48,3584]{1,0:T(8,128)(2,1)S(1)} collective-permute-done((bf16[48,3584]{1,0:T(8,128)(2,1)S(1)}, bf16[48,3584]{1,0:T(8,128)(2,1)S(1)}, u32[]{:S(2)}, u32[]{:S(2)}) %collective-permute-start.22) | collective-permute-done | bytes 344096 | tf_op jit(solution)/shard_map/ppermute | solution.py:24
  211.3 2.9 %collective-permute-start.28 = (bf16[2,2,24,3584]{3,2,0,1:T(8,128)(2,1)S(1)}, bf16[2,2,24,3584]{3,2,0,1:T(8,128)(2,1)S(1)}, u32[]{:S(2)}, u32[]{:S(2)}) collective-permute-start(bf16[2,2,24,3584]{3,2,0,1:T(8,128)(2,1)S(1)} %pad_maximum_fusion.7), channel_id=1, source_target_pairs={{0,24},{2,26},{4,28},{6,30},{1,25},{3,27},{5,29},{7,31},{8,0},{10,... | collective-permute-start | bytes 2064392 | tf_op jit(solution)/shard_map/ppermute | solution.py:24
  216.0 2.8 collective-permute-done.25
  224.7 4.8 %collective-permute-done.29 = bf16[2,2,24,3584]{3,2,1,0:T(8,128)(2,1)S(1)} collective-permute-done((bf16[2,2,24,3584]{3,2,1,0:T(8,128)(2,1)S(1)}, bf16[2,2,24,3584]{3,2,1,0:T(8,128)(2,1)S(1)}, u32[]{:S(2)}, u32[]{:S(2)}) %collective-permute-start.29) | collective-permute-done | bytes 688160 | tf_op jit(solution)/shard_map/ppermute | solution.py:24
  229.5 4.4 %collective-permute-done.26 = bf16[64,3584]{1,0:T(8,128)(2,1)S(1)} collective-permute-done((bf16[64,3584]{1,0:T(8,128)(2,1)S(1)}, bf16[64,3584]{1,0:T(8,128)(2,1)S(1)}, u32[]{:S(2)}, u32[]{:S(2)}) %collective-permute-start.26) | collective-permute-done | bytes 458784 | tf_op jit(solution)/shard_map/ppermute | solution.py:24
  242.4 4.6 %fusion.7 = bf16[1,1,3584,512]{3,2,1,0:T(8,128)(2,1)} fusion(bf16[768,3584]{1,0:T(8,128)(2,1)S(1)} %constant_dynamic-update-slice_fusion.85, bf16[768,512]{1,0:T(8,128)(2,1)S(1)} %constant_dynamic-update-slice_fusion.89), kind=kOutput, calls=%fused_computation.10 | convolution fusion | flops 2820407296 | bytes 9961472 | tf_op jit(solution)/shard_map/dot_general | solution.py:80
  247.0 5.4 %collective-permute-done.30 = bf16[2,2,24,3584]{3,2,1,0:T(8,128)(2,1)S(1)} collective-permute-done((bf16[2,2,24,3584]{3,2,1,0:T(8,128)(2,1)S(1)}, bf16[2,2,24,3584]{3,2,1,0:T(8,128)(2,1)S(1)}, u32[]{:S(2)}, u32[]{:S(2)}) %collective-permute-start.30) | collective-permute-done | bytes 688160 | tf_op jit(solution)/shard_map/ppermute | solution.py:24
  252.8 4.6 %collective-permute-done.34 = bf16[128,3584]{1,0:T(8,128)(2,1)S(1)} collective-permute-done((bf16[128,3584]{1,0:T(8,128)(2,1)S(1)}, bf16[128,3584]{1,0:T(8,128)(2,1)S(1)}, u32[]{:S(2)}, u32[]{:S(2)}) %collective-permute-start.34) | collective-permute-done | bytes 917536 | tf_op jit(solution)/shard_map/ppermute | solution.py:24
  258.1 3.0 %collective-permute-start.36 = (bf16[128,3584]{1,0:T(8,128)(2,1)S(1)}, bf16[128,3584]{1,0:T(8,128)(2,1)S(1)}, u32[]{:S(2)}, u32[]{:S(2)}) collective-permute-start(bf16[128,3584]{1,0:T(8,128)(2,1)S(1)} %fusion.18), channel_id=1, source_target_pairs={{32,0},{64,32},{96,64},{33,1},{65,33},{97,65},{34,2},{66,34},{98,6... | collective-permute-start | bytes 2752520 | tf_op jit(solution)/shard_map/ppermute | solution.py:46
  264.0 4.6 %fusion.8 = bf16[1,1,3584,512]{3,2,1,0:T(8,128)(2,1)} fusion(bf16[768,3584]{1,0:T(8,128)(2,1)S(1)} %constant_dynamic-update-slice_fusion.85, bf16[768,512]{1,0:T(8,128)(2,1)S(1)} %constant_dynamic-update-slice_fusion.105), kind=kOutput, calls=%fused_computation.11 | convolution fusion | flops 2820407296 | bytes 9961472 | tf_op jit(solution)/shard_map/dot_general | solution.py:80
  268.6 10.0 %collective-permute-done.36 = bf16[128,3584]{1,0:T(8,128)(2,1)S(1)} collective-permute-done((bf16[128,3584]{1,0:T(8,128)(2,1)S(1)}, bf16[128,3584]{1,0:T(8,128)(2,1)S(1)}, u32[]{:S(2)}, u32[]{:S(2)}) %collective-permute-start.36) | collective-permute-done | bytes 917536 | tf_op jit(solution)/shard_map/ppermute | solution.py:46
  278.6 6.1 %collective-permute-done.33 = bf16[128,3584]{1,0:T(8,128)(2,1)S(1)} collective-permute-done((bf16[128,3584]{1,0:T(8,128)(2,1)S(1)}, bf16[128,3584]{1,0:T(8,128)(2,1)S(1)}, u32[]{:S(2)}, u32[]{:S(2)}) %collective-permute-start.33) | collective-permute-done | bytes 917536 | tf_op jit(solution)/shard_map/ppermute | solution.py:46
  (393 shorter events, 90.2 us)
Async XLA Ops:
  5.8 26.7 %collective-permute-start.1 = (bf16[136,3584]{1,0:T(8,128)(2,1)}, bf16[136,3584]{1,0:T(8,128)(2,1)}, u32[]{:S(2)}, u32[]{:S(2)}) collective-permute-start(bf16[136,3584]{1,0:T(8,128)(2,1)} %fusion.21), channel_id=1, source_target_pairs={{0,4},{2,6},{4,1},{6,3},{1,5},{3,7},{5,0},{7,2},{8,12},{10,14},{12... | collective-permute-start | bytes 2924552 | tf_op jit(solution)/shard_map/ppermute | solution.py:24
  7.7 24.7 %collective-permute-start.2 = (bf16[136,3584]{1,0:T(8,128)(2,1)}, bf16[136,3584]{1,0:T(8,128)(2,1)}, u32[]{:S(2)}, u32[]{:S(2)}) collective-permute-start(bf16[136,3584]{1,0:T(8,128)(2,1)} %fusion.21), channel_id=1, source_target_pairs={{0,5},{2,7},{4,0},{6,2},{1,4},{3,6},{5,1},{7,3},{8,13},{10,15},{12... | collective-permute-start | bytes 2924552 | tf_op jit(solution)/shard_map/ppermute | solution.py:24
  12.5 19.9 %collective-permute-start.3 = (bf16[96,3584]{1,0:T(8,128)(2,1)S(1)}, bf16[96,3584]{1,0:T(8,128)(2,1)S(1)}, u32[]{:S(2)}, u32[]{:S(2)}) collective-permute-start(bf16[96,3584]{1,0:T(8,128)(2,1)S(1)} %pad_maximum_fusion.4), channel_id=1, source_target_pairs={{0,8},{2,10},{4,12},{6,14},{1,9},{3,11},{5,13},{7,15},{8,16},{10,1... | collective-permute-start | bytes 2064392 | tf_op jit(solution)/shard_map/ppermute | solution.py:24
  14.2 18.2 %collective-permute-start.4 = (bf16[96,3584]{1,0:T(8,128)(2,1)S(1)}, bf16[96,3584]{1,0:T(8,128)(2,1)S(1)}, u32[]{:S(2)}, u32[]{:S(2)}) collective-permute-start(bf16[96,3584]{1,0:T(8,128)(2,1)S(1)} %pad_maximum_fusion.5), channel_id=1, source_target_pairs={{0,24},{2,26},{4,28},{6,30},{1,25},{3,27},{5,29},{7,31},{8,0},{10,... | collective-permute-start | bytes 2064392 | tf_op jit(solution)/shard_map/ppermute | solution.py:24
  34.2 13.9 %collective-permute-start.6 = (bf16[72,3584]{1,0:T(8,128)(2,1)S(1)}, bf16[72,3584]{1,0:T(8,128)(2,1)S(1)}, u32[]{:S(2)}, u32[]{:S(2)}) collective-permute-start(bf16[72,3584]{1,0:T(8,128)(2,1)S(1)} %slice.821), channel_id=1, source_target_pairs={{0,5},{2,7},{4,0},{6,2},{1,4},{3,6},{5,1},{7,3},{8,13},{10,15},{12... | collective-permute-start | bytes 1548296 | tf_op jit(solution)/shard_map/ppermute | solution.py:24
  39.6 13.1 %collective-permute-start.5 = (bf16[64,3584]{1,0:T(8,128)(2,1)S(1)}, bf16[64,3584]{1,0:T(8,128)(2,1)S(1)}, u32[]{:S(2)}, u32[]{:S(2)}) collective-permute-start(bf16[64,3584]{1,0:T(8,128)(2,1)S(1)} %slice.820), channel_id=1, source_target_pairs={{0,4},{2,6},{4,1},{6,3},{1,5},{3,7},{5,0},{7,2},{8,12},{10,14},{12... | collective-permute-start | bytes 1376264 | tf_op jit(solution)/shard_map/ppermute | solution.py:24
  39.6 18.6 %collective-permute-start.7 = (bf16[96,3584]{1,0:T(8,128)(2,1)S(1)}, bf16[96,3584]{1,0:T(8,128)(2,1)S(1)}, u32[]{:S(2)}, u32[]{:S(2)}) collective-permute-start(bf16[96,3584]{1,0:T(8,128)(2,1)S(1)} %pad_maximum_fusion.6), channel_id=1, source_target_pairs={{0,16},{2,18},{4,20},{6,22},{1,17},{3,19},{5,21},{7,23},{8,24},{10... | collective-permute-start | bytes 2064392 | tf_op jit(solution)/shard_map/ppermute | solution.py:24
  58.5 31.9 %collective-permute-start.8 = (bf16[192,3584]{1,0:T(8,128)(2,1)S(1)}, bf16[192,3584]{1,0:T(8,128)(2,1)S(1)}, u32[]{:S(2)}, u32[]{:S(2)}) collective-permute-start(bf16[192,3584]{1,0:T(8,128)(2,1)S(1)} %get-tuple-element.356), channel_id=1, source_target_pairs={{0,4},{2,6},{4,1},{6,3},{1,5},{3,7},{5,0},{7,2},{8,12},{10,14},{12... | collective-permute-start | bytes 4128776 | tf_op jit(solution)/shard_map/ppermute | solution.py:24
  58.5 31.8 %collective-permute-start.9 = (bf16[192,3584]{1,0:T(8,128)(2,1)S(1)}, bf16[192,3584]{1,0:T(8,128)(2,1)S(1)}, u32[]{:S(2)}, u32[]{:S(2)}) collective-permute-start(bf16[192,3584]{1,0:T(8,128)(2,1)S(1)} %get-tuple-element.356), channel_id=1, source_target_pairs={{0,5},{2,7},{4,0},{6,2},{1,4},{3,6},{5,1},{7,3},{8,13},{10,15},{12... | collective-permute-start | bytes 4128776 | tf_op jit(solution)/shard_map/ppermute | solution.py:24
  67.7 33.6 %collective-permute-start.11 = (bf16[192,3584]{1,0:T(8,128)(2,1)S(1)}, bf16[192,3584]{1,0:T(8,128)(2,1)S(1)}, u32[]{:S(2)}, u32[]{:S(2)}) collective-permute-start(bf16[192,3584]{1,0:T(8,128)(2,1)S(1)} %bitcast.356), channel_id=1, source_target_pairs={{0,8},{2,10},{4,12},{6,14},{1,9},{3,11},{5,13},{7,15},{8,16},{10,1... | collective-permute-start | bytes 4128776 | tf_op jit(solution)/shard_map/ppermute | solution.py:24
  69.3 31.9 %collective-permute-start.12 = (bf16[192,3584]{1,0:T(8,128)(2,1)S(1)}, bf16[192,3584]{1,0:T(8,128)(2,1)S(1)}, u32[]{:S(2)}, u32[]{:S(2)}) collective-permute-start(bf16[192,3584]{1,0:T(8,128)(2,1)S(1)} %bitcast.355), channel_id=1, source_target_pairs={{0,24},{2,26},{4,28},{6,30},{1,25},{3,27},{5,29},{7,31},{8,0},{10,... | collective-permute-start | bytes 4128776 | tf_op jit(solution)/shard_map/ppermute | solution.py:24
  102.5 33.1 %collective-permute-start.14 = (bf16[192,3584]{1,0:T(8,128)(2,1)S(1)}, bf16[192,3584]{1,0:T(8,128)(2,1)}, u32[]{:S(2)}, u32[]{:S(2)}) collective-permute-start(bf16[192,3584]{1,0:T(8,128)(2,1)S(1)} %get-tuple-element.214.refs_2_), channel_id=1, source_target_pairs={{0,1},{2,3},{4,5},{6,7},{1,0},{3,2},{5,4},{7,6},{8,9},{10,11},{12,... | collective-permute-start | bytes 4128776 | tf_op jit(solution)/shard_map/ppermute | solution.py:24
  103.3 33.0 %collective-permute-start.15 = (bf16[192,3584]{1,0:T(8,128)(2,1)}, bf16[192,3584]{1,0:T(8,128)(2,1)}, u32[]{:S(2)}, u32[]{:S(2)}) collective-permute-start(bf16[192,3584]{1,0:T(8,128)(2,1)} %bitcast.61), channel_id=1, source_target_pairs={{0,16},{2,18},{4,20},{6,22},{1,17},{3,19},{5,21},{7,23},{8,24},{10... | collective-permute-start | bytes 4128776 | tf_op jit(solution)/shard_map/ppermute | solution.py:24
  136.3 30.6 %collective-permute-start.16 = (bf16[192,3584]{1,0:T(8,128)(2,1)}, bf16[192,3584]{1,0:T(8,128)(2,1)}, u32[]{:S(2)}, u32[]{:S(2)}) collective-permute-start(bf16[192,3584]{1,0:T(8,128)(2,1)} %get-tuple-element.173), channel_id=1, source_target_pairs={{0,5},{2,7},{4,0},{6,2},{1,4},{3,6},{5,1},{7,3},{8,13},{10,15},{12... | collective-permute-start | bytes 4128776 | tf_op jit(solution)/shard_map/ppermute | solution.py:24
  137.1 31.6 %collective-permute-start.17 = (bf16[192,3584]{1,0:T(8,128)(2,1)}, bf16[192,3584]{1,0:T(8,128)(2,1)}, u32[]{:S(2)}, u32[]{:S(2)}) collective-permute-start(bf16[192,3584]{1,0:T(8,128)(2,1)} %get-tuple-element.174), channel_id=1, source_target_pairs={{0,4},{2,6},{4,1},{6,3},{1,5},{3,7},{5,0},{7,2},{8,12},{10,14},{12... | collective-permute-start | bytes 4128776 | tf_op jit(solution)/shard_map/ppermute | solution.py:24
  138.3 22.9 %collective-permute-start.18 = (bf16[144,3584]{1,0:T(8,128)(2,1)}, bf16[144,3584]{1,0:T(8,128)(2,1)}, u32[]{:S(2)}, u32[]{:S(2)}) collective-permute-start(bf16[144,3584]{1,0:T(8,128)(2,1)} %get-tuple-element.175), channel_id=1, source_target_pairs={{0,24},{2,26},{4,28},{6,30},{1,25},{3,27},{5,29},{7,31},{8,0},{10,... | collective-permute-start | bytes 3096584 | tf_op jit(solution)/shard_map/ppermute | solution.py:24
  141.1 23.3 %collective-permute-start.19 = (bf16[144,3584]{1,0:T(8,128)(2,1)}, bf16[144,3584]{1,0:T(8,128)(2,1)}, u32[]{:S(2)}, u32[]{:S(2)}) collective-permute-start(bf16[144,3584]{1,0:T(8,128)(2,1)} %get-tuple-element.176), channel_id=1, source_target_pairs={{0,8},{2,10},{4,12},{6,14},{1,9},{3,11},{5,13},{7,15},{8,16},{10,1... | collective-permute-start | bytes 3096584 | tf_op jit(solution)/shard_map/ppermute | solution.py:24
  168.9 39.1 %collective-permute-start.20 = (bf16[192,3584]{1,0:T(8,128)(2,1)S(1)}, bf16[192,3584]{1,0:T(8,128)(2,1)S(1)}, u32[]{:S(2)}, u32[]{:S(2)}) collective-permute-start(bf16[192,3584]{1,0:T(8,128)(2,1)S(1)} %get-tuple-element.192), channel_id=1, source_target_pairs={{0,1},{2,3},{4,5},{6,7},{1,0},{3,2},{5,4},{7,6},{8,9},{10,11},{12,... | collective-permute-start | bytes 4128776 | tf_op jit(solution)/shard_map/ppermute | solution.py:24
  170.3 37.7 %collective-permute-start.21 = (bf16[192,3584]{1,0:T(8,128)(2,1)S(1)}, bf16[192,3584]{1,0:T(8,128)(2,1)S(1)}, u32[]{:S(2)}, u32[]{:S(2)}) collective-permute-start(bf16[192,3584]{1,0:T(8,128)(2,1)S(1)} %get-tuple-element.194), channel_id=1, source_target_pairs={{0,16},{2,18},{4,20},{6,22},{1,17},{3,19},{5,21},{7,23},{8,24},{10... | collective-permute-start | bytes 4128776 | tf_op jit(solution)/shard_map/ppermute | solution.py:24
  172.4 35.6 %collective-permute-start.24 = (bf16[96,3584]{1,0:T(8,128)(2,1)S(1)}, bf16[96,3584]{1,0:T(8,128)(2,1)S(1)}, u32[]{:S(2)}, u32[]{:S(2)}) collective-permute-start(bf16[96,3584]{1,0:T(8,128)(2,1)S(1)} %slice.905), channel_id=1, source_target_pairs={{0,2},{2,0},{4,6},{6,4},{1,3},{3,1},{5,7},{7,5},{8,10},{10,8},{12,... | collective-permute-start | bytes 2064392 | tf_op jit(solution)/shard_map/ppermute | solution.py:24
  172.4 35.2 %collective-permute-start.22 = (bf16[48,3584]{1,0:T(8,128)(2,1)S(1)}, bf16[48,3584]{1,0:T(8,128)(2,1)S(1)}, u32[]{:S(2)}, u32[]{:S(2)}) collective-permute-start(bf16[48,3584]{1,0:T(8,128)(2,1)S(1)} %get-tuple-element.195), channel_id=1, source_target_pairs={{0,24},{2,26},{4,28},{6,30},{1,25},{3,27},{5,29},{7,31},{8,0},{10,... | collective-permute-start | bytes 1032200 | tf_op jit(solution)/shard_map/ppermute | solution.py:24
  173.7 34.2 %collective-permute-start.23 = (bf16[48,3584]{1,0:T(8,128)(2,1)S(1)}, bf16[48,3584]{1,0:T(8,128)(2,1)S(1)}, u32[]{:S(2)}, u32[]{:S(2)}) collective-permute-start(bf16[48,3584]{1,0:T(8,128)(2,1)S(1)} %get-tuple-element.196), channel_id=1, source_target_pairs={{0,8},{2,10},{4,12},{6,14},{1,9},{3,11},{5,13},{7,15},{8,16},{10,1... | collective-permute-start | bytes 1032200 | tf_op jit(solution)/shard_map/ppermute | solution.py:24
  210.9 18.7 %collective-permute-start.29 = (bf16[2,2,24,3584]{3,2,1,0:T(8,128)(2,1)S(1)}, bf16[2,2,24,3584]{3,2,1,0:T(8,128)(2,1)S(1)}, u32[]{:S(2)}, u32[]{:S(2)}) collective-permute-start(bf16[2,2,24,3584]{3,2,1,0:T(8,128)(2,1)S(1)} %pad_maximum_fusion.8), channel_id=1, source_target_pairs={{0,8},{2,10},{4,12},{6,14},{1,9},{3,11},{5,13},{7,15},{8,16},{10,1... | collective-permute-start | bytes 2064392 | tf_op jit(solution)/shard_map/ppermute | solution.py:24
  211.3 18.2 %collective-permute-start.28 = (bf16[2,2,24,3584]{3,2,0,1:T(8,128)(2,1)S(1)}, bf16[2,2,24,3584]{3,2,0,1:T(8,128)(2,1)S(1)}, u32[]{:S(2)}, u32[]{:S(2)}) collective-permute-start(bf16[2,2,24,3584]{3,2,0,1:T(8,128)(2,1)S(1)} %pad_maximum_fusion.7), channel_id=1, source_target_pairs={{0,24},{2,26},{4,28},{6,30},{1,25},{3,27},{5,29},{7,31},{8,0},{10,... | collective-permute-start | bytes 2064392 | tf_op jit(solution)/shard_map/ppermute | solution.py:24
  220.1 13.8 %collective-permute-start.26 = (bf16[64,3584]{1,0:T(8,128)(2,1)S(1)}, bf16[64,3584]{1,0:T(8,128)(2,1)S(1)}, u32[]{:S(2)}, u32[]{:S(2)}) collective-permute-start(bf16[64,3584]{1,0:T(8,128)(2,1)S(1)} %get-tuple-element.350), channel_id=1, source_target_pairs={{0,4},{2,6},{4,1},{6,3},{1,5},{3,7},{5,0},{7,2},{8,12},{10,14},{12... | collective-permute-start | bytes 1376264 | tf_op jit(solution)/shard_map/ppermute | solution.py:24
  220.9 13.1 %collective-permute-start.27 = (bf16[64,3584]{1,0:T(8,128)(2,1)S(1)}, bf16[64,3584]{1,0:T(8,128)(2,1)S(1)}, u32[]{:S(2)}, u32[]{:S(2)}) collective-permute-start(bf16[64,3584]{1,0:T(8,128)(2,1)S(1)} %get-tuple-element.349), channel_id=1, source_target_pairs={{0,5},{2,7},{4,0},{6,2},{1,4},{3,6},{5,1},{7,3},{8,13},{10,15},{12... | collective-permute-start | bytes 1376264 | tf_op jit(solution)/shard_map/ppermute | solution.py:24
  234.1 18.2 %collective-permute-start.30 = (bf16[2,2,24,3584]{3,2,1,0:T(8,128)(2,1)S(1)}, bf16[2,2,24,3584]{3,2,1,0:T(8,128)(2,1)S(1)}, u32[]{:S(2)}, u32[]{:S(2)}) collective-permute-start(bf16[2,2,24,3584]{3,2,1,0:T(8,128)(2,1)S(1)} %pad_maximum_fusion.9), channel_id=1, source_target_pairs={{0,16},{2,18},{4,20},{6,22},{1,17},{3,19},{5,21},{7,23},{8,24},{10... | collective-permute-start | bytes 2064392 | tf_op jit(solution)/shard_map/ppermute | solution.py:24
  234.8 22.6 %collective-permute-start.34 = (bf16[128,3584]{1,0:T(8,128)(2,1)S(1)}, bf16[128,3584]{1,0:T(8,128)(2,1)S(1)}, u32[]{:S(2)}, u32[]{:S(2)}) collective-permute-start(bf16[128,3584]{1,0:T(8,128)(2,1)S(1)} %pad_maximum_fusion.1), channel_id=1, source_target_pairs={{0,4},{2,6},{4,1},{6,3},{1,5},{3,7},{5,0},{7,2},{8,12},{10,14},{12... | collective-permute-start | bytes 2752520 | tf_op jit(solution)/shard_map/ppermute | solution.py:24
  235.9 21.5 %collective-permute-start.35 = (bf16[128,3584]{1,0:T(8,128)(2,1)S(1)}, bf16[128,3584]{1,0:T(8,128)(2,1)S(1)}, u32[]{:S(2)}, u32[]{:S(2)}) collective-permute-start(bf16[128,3584]{1,0:T(8,128)(2,1)S(1)} %pad_maximum_fusion.2), channel_id=1, source_target_pairs={{0,5},{2,7},{4,0},{6,2},{1,4},{3,6},{5,1},{7,3},{8,13},{10,15},{12... | collective-permute-start | bytes 2752520 | tf_op jit(solution)/shard_map/ppermute | solution.py:24
  238.6 22.5 %collective-permute-start.31 = (bf16[3,2,24,3584]{3,2,1,0:T(8,128)(2,1)S(1)}, bf16[3,2,24,3584]{3,2,1,0:T(8,128)(2,1)S(1)}, u32[]{:S(2)}, u32[]{:S(2)}) collective-permute-start(bf16[3,2,24,3584]{3,2,1,0:T(8,128)(2,1)S(1)} %pad_maximum_fusion), channel_id=1, source_target_pairs={{0,2},{2,0},{4,6},{6,4},{1,3},{3,1},{5,7},{7,5},{8,10},{10,8},{12,... | collective-permute-start | bytes 3096584 | tf_op jit(solution)/shard_map/ppermute | solution.py:24
  258.1 20.5 %collective-permute-start.36 = (bf16[128,3584]{1,0:T(8,128)(2,1)S(1)}, bf16[128,3584]{1,0:T(8,128)(2,1)S(1)}, u32[]{:S(2)}, u32[]{:S(2)}) collective-permute-start(bf16[128,3584]{1,0:T(8,128)(2,1)S(1)} %fusion.18), channel_id=1, source_target_pairs={{32,0},{64,32},{96,64},{33,1},{65,33},{97,65},{34,2},{66,34},{98,6... | collective-permute-start | bytes 2752520 | tf_op jit(solution)/shard_map/ppermute | solution.py:46
  262.7 21.9 %collective-permute-start.33 = (bf16[128,3584]{1,0:T(8,128)(2,1)S(1)}, bf16[128,3584]{1,0:T(8,128)(2,1)S(1)}, u32[]{:S(2)}, u32[]{:S(2)}) collective-permute-start(bf16[128,3584]{1,0:T(8,128)(2,1)S(1)} %fusion.19), channel_id=1, source_target_pairs={{0,32},{32,64},{64,96},{1,33},{33,65},{65,97},{2,34},{34,66},{66,9... | collective-permute-start | bytes 2752520 | tf_op jit(solution)/shard_map/ppermute | solution.py:46
  (81 other events, 651.4 us)
where the time goes:
time: 288 us; the launch traced here: 286 us
  waiting for transfers between devices  133 us (46%)
  starting transfers between devices  50.2 us (17%)
  Pallas kernels  36 us (12%)
  local copies, waits for them, and re-layouts  30.4 us (11%)
  matrix products  26.2 us (9%)
  other arithmetic  8.52 us (3%)
    ppermute x35, waiting for transfers between devices, shifted(): return lax.ppermute(x, GROUP, pairs)  116 us
    ppermute x35, starting transfers between devices, shifted(): return lax.ppermute(x, GROUP, pairs)  45.9 us
    dot_general x9, matrix products, mm_first(): lax.dot_general(a, b, (((0,), (0,)), ((), ())), preferred_element_type=F32)  21.6 us
    unnamed x219, local copies, waits for them, and re-layouts  20.7 us
    ppermute x2, waiting for transfers between devices, from_behind(): return lax.ppermute(x, axis, pairs)  16 us
    pallas_call x2, Pallas kernels, backward(): kernel_call(body, 7, [whole(a) for a in operands] + [rows_block(n, units)...  12.8 us
    pallas_call x2, Pallas kernels, forward(): kernel_call(body, 2, [whole(x) for x in pieces] + [columns(depth, n)] * 2...  8.99 us
    pallas_call x2, Pallas kernels, outputs(): kernel_call(body, 7, [whole(h) for h in hidden] + [columns(units, n)], [c...  7.49 us
  transfers between devices with their start and end apart: 37, of which 20 were waited for; matrix products, arithmetic and copies ran while one was open for 15% of the time, Pallas kernels for 13%

commit v1 on v0

--- a/solution.py
+++ b/solution.py
@@ -359,6 +359,14 @@
     far1, far3 = [a.reshape(2, 1, slot, width) for a in (far1, far3)]
     others = swap_core(jnp.concatenate([b2[1], b1[1], b3[1], far1[1], far3[1]]))
 
+    both = [
+        (out0.astype(F32) + e2.astype(F32)).astype(BF).reshape(4, 2, slot, width),
+        (e1.astype(F32) + e3.astype(F32)).astype(BF).reshape(4, 2, slot, width),
+    ]
+    both, others = lax.optimization_barrier(
+        ([jnp.stack([a[t] for a in both]) for t in range(4)], others)
+    )
+
     def in_order(whole0, part1, whole2, part3, rest1, rest3):
         part1, part3 = [[p[0], p[1], r[0], p[2]] for p, r in ((part1, rest1), (part3, rest3))]
         return [whole0, part1, whole2, part3]
@@ -372,11 +380,6 @@
         rows_of = jnp.stack([back[dc][t][s] for dc in range(2) for t in range(4)])
         return mm(pick_z[s], rows_of.reshape(-1, width))
 
-    both = [
-        (out0.astype(F32) + e2.astype(F32)).astype(BF).reshape(4, 2, slot, width),
-        (e1.astype(F32) + e3.astype(F32)).astype(BF).reshape(4, 2, slot, width),
-    ]
-    both = [jnp.stack([a[t] for a in both]) for t in range(4)]
     m1, m3 = shift_y(both[1], -1), shift_y(both[3], -3)
     far = by_token(2).astype(BF)
     far_a, far_b = shift_z(far[:split], 1), shift_z(far[split:], -1)

time: 288 us -> 295 us (1.024)
  local copies, waits for them, and re-layouts: 30.4 us -> 38.4 us
  starting transfers between devices: 50.2 us -> 45.4 us
    unnamed x219 -> x259, local copies, waits for them, and re-layouts: 20.7 us -> 27.2 us
    ppermute x35, starting transfers between devices: 45.9 us -> 41 us  [shifted(): return lax.ppermute(x, GROUP, pairs)]
  transfers between devices with their start and end apart: 37 -> 37, of which waited for: 20 -> 22; matrix products, arithmetic and copies ran while one was open for 15% -> 14% of each run, Pallas kernels for 13% -> 12%
where the time goes in v1:
time: 295 us; the launch traced here: 293 us
  waiting for transfers between devices  135 us (46%)
  starting transfers between devices  45.4 us (15%)
  local copies, waits for them, and re-layouts  38.4 us (13%)
  Pallas kernels  36 us (12%)
  matrix products  26.2 us (9%)
  other arithmetic  9.22 us (3%)
    ppermute x35, waiting for transfers between devices, shifted(): return lax.ppermute(x, GROUP, pairs)  118 us
    ppermute x35, starting transfers between devices, shifted(): return lax.ppermute(x, GROUP, pairs)  41 us
    unnamed x259, local copies, waits for them, and re-layouts  27.2 us
    dot_general x9, matrix products, mm_first(): lax.dot_general(a, b, (((0,), (0,)), ((), ())), preferred_element_type=F32)  21.6 us
    ppermute x2, waiting for transfers between devices, from_behind(): return lax.ppermute(x, axis, pairs)  17.7 us
    pallas_call x2, Pallas kernels, backward(): kernel_call(body, 7, [whole(a) for a in operands] + [rows_block(n, units)...  12.6 us
    pallas_call x2, Pallas kernels, forward(): kernel_call(body, 2, [whole(x) for x in pieces] + [columns(depth, n)] * 2...  9.14 us
    pallas_call x2, Pallas kernels, outputs(): kernel_call(body, 7, [whole(h) for h in hidden] + [columns(units, n)], [c...  7.48 us
  transfers between devices with their start and end apart: 37, of which 22 were waited for; matrix products, arithmetic and copies ran while one was open for 14% of the time, Pallas kernels for 12%

profile of v1, /device:TPU:6, one launch (start us, length us, event | category | flops | bytes accessed | tf_op | source)
XLA Modules:
  0.0 293.1 jit_solution(3402356054689096448)
XLA Ops:
  6.4 4.1 %collective-permute-start.2 = (bf16[136,3584]{1,0:T(8,128)(2,1)}, bf16[136,3584]{1,0:T(8,128)(2,1)}, u32[]{:S(2)}, u32[]{:S(2)}) collective-permute-start(bf16[136,3584]{1,0:T(8,128)(2,1)} %fusion.19), channel_id=1, source_target_pairs={{0,5},{2,7},{4,0},{6,2},{1,4},{3,6},{5,1},{7,3},{8,13},{10,15},{12... | collective-permute-start | bytes 2924552 | tf_op jit(solution)/shard_map/ppermute | solution.py:24
  11.8 2.2 collective-permute-done
  19.8 11.9 %collective-permute-done.2 = bf16[136,3584]{1,0:T(8,128)(2,1)} collective-permute-done((bf16[136,3584]{1,0:T(8,128)(2,1)}, bf16[136,3584]{1,0:T(8,128)(2,1)}, u32[]{:S(2)}, u32[]{:S(2)}) %collective-permute-start.2) | collective-permute-done | bytes 974880 | tf_op jit(solution)/shard_map/ppermute | solution.py:24
  31.7 3.4 %collective-permute-done.1 = bf16[136,3584]{1,0:T(8,128)(2,1)} collective-permute-done((bf16[136,3584]{1,0:T(8,128)(2,1)}, bf16[136,3584]{1,0:T(8,128)(2,1)}, u32[]{:S(2)}, u32[]{:S(2)}) %collective-permute-start.1) | collective-permute-done | bytes 974880 | tf_op jit(solution)/shard_map/ppermute | solution.py:24
  39.2 3.3 %collective-permute-start.6 = (bf16[72,3584]{1,0:T(8,128)(2,1)S(1)}, bf16[72,3584]{1,0:T(8,128)(2,1)S(1)}, u32[]{:S(2)}, u32[]{:S(2)}) collective-permute-start(bf16[72,3584]{1,0:T(8,128)(2,1)S(1)} %slice.821), channel_id=1, source_target_pairs={{0,5},{2,7},{4,0},{6,2},{1,4},{3,6},{5,1},{7,3},{8,13},{10,15},{12... | collective-permute-start | bytes 1548296 | tf_op jit(solution)/shard_map/ppermute | solution.py:24
  42.5 3.3 %collective-permute-start.7 = (bf16[96,3584]{1,0:T(8,128)(2,1)S(1)}, bf16[96,3584]{1,0:T(8,128)(2,1)S(1)}, u32[]{:S(2)}, u32[]{:S(2)}) collective-permute-start(bf16[96,3584]{1,0:T(8,128)(2,1)S(1)} %pad_maximum_fusion.6), channel_id=1, source_target_pairs={{0,16},{2,18},{4,20},{6,22},{1,17},{3,19},{5,21},{7,23},{8,24},{10... | collective-permute-start | bytes 2064392 | tf_op jit(solution)/shard_map/ppermute | solution.py:24
  45.8 6.3 %collective-permute-done.6 = bf16[72,3584]{1,0:T(8,128)(2,1)S(1)} collective-permute-done((bf16[72,3584]{1,0:T(8,128)(2,1)S(1)}, bf16[72,3584]{1,0:T(8,128)(2,1)S(1)}, u32[]{:S(2)}, u32[]{:S(2)}) %collective-permute-start.6) | collective-permute-done | bytes 516128 | tf_op jit(solution)/shard_map/ppermute | solution.py:24
  69.7 19.5 %collective-permute-done.9.refs_1_ = bf16[192,3584]{1,0:T(8,128)(2,1)S(1)} collective-permute-done((bf16[192,3584]{1,0:T(8,128)(2,1)S(1)}, bf16[192,3584]{1,0:T(8,128)(2,1)S(1)}, u32[]{:S(2)}, u32[]{:S(2)}) %collective-permute-start.9) | collective-permute-done | bytes 1376288 | tf_op jit(solution)/shard_map/ppermute | solution.py:24
  89.2 3.3 %collective-permute-done.8.refs_0_ = bf16[192,3584]{1,0:T(8,128)(2,1)S(1)} collective-permute-done((bf16[192,3584]{1,0:T(8,128)(2,1)S(1)}, bf16[192,3584]{1,0:T(8,128)(2,1)S(1)}, u32[]{:S(2)}, u32[]{:S(2)}) %collective-permute-start.8) | collective-permute-done | bytes 1376288 | tf_op jit(solution)/shard_map/ppermute | solution.py:24
  92.5 6.3 %collective-permute-done.11.refs_0_ = bf16[192,3584]{1,0:T(8,128)(2,1)S(1)} collective-permute-done((bf16[192,3584]{1,0:T(8,128)(2,1)S(1)}, bf16[192,3584]{1,0:T(8,128)(2,1)S(1)}, u32[]{:S(2)}, u32[]{:S(2)}) %collective-permute-start.11) | collective-permute-done | bytes 1376288 | tf_op jit(solution)/shard_map/ppermute | solution.py:24
  99.9 2.9 collective-permute-start.15
  104.6 5.4 %shard_map.110 = (f32[192,512]{1,0:T(8,128)S(1)}, f32[192,512]{1,0:T(8,128)S(1)}, bf16[192,512]{1,0:T(8,128)(2,1)S(1)}, f32[192,512]{1,0:T(8,128)S(1)}, f32[192,...) custom-call(bf16[192,3584]{1,0:T(8,128)(2,1)S(1)} %collective-permut, ...), custom_call_target="tpu_custom_call" | custom-call | flops 1 | bytes 1 | tf_op jit(solution)/shard_map/pallas_call | solution.py:123
  114.5 4.4 %shard_map.111 = (bf16[192,3584]{1,0:T(8,128)(2,1)}, bf16[192,3584]{1,0:T(8,128)(2,1)}) custom-call(bf16[192,512]{1,0:T(8,128)(2,1)S(1)} %get-tuple-element.264.refs_0_, bf16[192,512]{1,0:T(8,128)(2,1)S(1)} %get-tuple-element.266.refs_1_, bf16[512,3584]{1,0:T(8,128)(2,1)S(1)} %bitcast.310), custom_call_target="tpu_custom_call" | custom-call | flops 1 | bytes 1 | tf_op jit(solution)/shard_map/pallas_call | solution.py:142
  122.9 3.9 %shard_map.112 = (f32[192,512]{1,0:T(8,128)S(1)}, f32[192,512]{1,0:T(8,128)S(1)}, f32[192,512]{1,0:T(8,128)S(1)}) custom-call(bf16[192,3584]{1,0:T(8,128)(2,1)S(1)} %copy-done.32, bf16[192,3584]{1,0:T(8,128)(2,1)S(1)} %copy-done.35, bf16[192,3584]{1,0:T(8,128)(2,1)S(1)} %bitcast.314, bf16[512,3584]{1,0:T(8,128)(2,1)S(1)} %bitcast.311), custom_call_target="tpu_custom_call" | custom-call | flops 1 | bytes 1 | tf_op jit(solution)/shard_map/pallas_call | solution.py:160
  131.1 5.0 %shard_map.113 = (bf16[144,3584]{1,0:T(8,128)(2,1)S(1)}, bf16[144,3584]{1,0:T(8,128)(2,1)}, bf16[288,512]{1,0:T(8,128)(2,1)S(1)}, bf16[288,512]{1,0:T(8,128)(2,1)S(1)}) custom-call(f32[192,512]{1,0:T(8,128)S(1)} %copy-done.20, f32[192,512]{1,0:T(8,128)S(1)} %get-tuple-element.167.refs_1_, f32[192,512]{1,0:T(8,128)S(1)} %copy-done.16, ...), custom_call_target="tpu_custom_call" | custom-call | flops 1 | bytes 1 | tf_op jit(solution)/shard_map/pallas_call | solution.py:214
  142.6 2.9 shard_map.116.refs_9_
  145.5 3.8 %shard_map.114 = (f32[192,512]{1,0:T(8,128)S(1)}, f32[192,512]{1,0:T(8,128)S(1)}, bf16[192,512]{1,0:T(8,128)(2,1)S(1)}) custom-call(bf16[192,3584]{1,0:T(8,128)(2,1)} %collective-permute-done.14.refs_0_, bf16[3584,512]{1,0:T(8,128)(2,1)S(1)} %bitcast.304, bf16[3584,512]{1,0:T(8,128)(2,1)S(1)} %bitcast.309), custom_call_target="tpu_custom_call" | custom-call | flops 1 | bytes 1 | tf_op jit(solution)/shard_map/pallas_call | solution.py:123
  149.4 3.1 %shard_map.115 = (bf16[192,3584]{1,0:T(8,128)(2,1)S(1)}, bf16[192,3584]{1,0:T(8,128)(2,1)S(1)}) custom-call(bf16[192,512]{1,0:T(8,128)(2,1)S(1)} %get-tuple-element.265.refs_0_, bf16[192,512]{1,0:T(8,128)(2,1)S(1)} %copy-done.40, bf16[512,3584]{1,0:T(8,128)(2,1)S(1)} %bitcast.313), custom_call_target="tpu_custom_call" | custom-call | flops 1 | bytes 1 | tf_op jit(solution)/shard_map/pallas_call | solution.py:142
  152.5 7.7 %shard_map.117 = (bf16[192,3584]{1,0:T(8,128)(2,1)S(1)}, bf16[192,3584]{1,0:T(8,128)(2,1)S(1)}, bf16[48,3584]{1,0:T(8,128)(2,1)S(1)}, bf16[48,3584]{1,0:T(8,128)...) custom-call(f32[192,512]{1,0:T(8,128)S(1)} %copy-done.21, ...), custom_call_target="tpu_custom_call" | custom-call | flops 1 | bytes 1 | tf_op jit(solution)/shard_map/pallas_call | solution.py:214
  163.9 3.5 %collective-permute-done.16 = bf16[192,3584]{1,0:T(8,128)(2,1)} collective-permute-done((bf16[192,3584]{1,0:T(8,128)(2,1)}, bf16[192,3584]{1,0:T(8,128)(2,1)}, u32[]{:S(2)}, u32[]{:S(2)}) %collective-permute-start.16) | collective-permute-done | bytes 1376288 | tf_op jit(solution)/shard_map/ppermute | solution.py:24
  175.5 5.6 %fusion.9 = bf16[1,1,512,3584]{3,2,1,0:T(8,128)(2,1)} fusion(bf16[768,512]{1,0:T(8,128)(2,1)S(1)} %bitcast.353, bf16[192,3584]{1,0:T(8,128)(2,1)S(1)} %copy-done.36, bf16[192,3584]{1,0:T(8,128)(2,1)} %collective-permute-done.15.refs_0_, bf16[192,3584]{1,0:T(8,128)(2,1)S(1)} %copy-done.33, bf16[192,3584]{1,0:T(8,128)(2,1)S(1)} %bitcast.315), kind=kOutput, calls=%fused_computation.12 | convolution fusion | flops 2842427392 | bytes 9961472 | tf_op jit(solution)/shard_map/dot_general | solution.py:80
  183.3 25.7 %collective-permute-done.23 = bf16[48,3584]{1,0:T(8,128)(2,1)S(1)} collective-permute-done((bf16[48,3584]{1,0:T(8,128)(2,1)S(1)}, bf16[48,3584]{1,0:T(8,128)(2,1)S(1)}, u32[]{:S(2)}, u32[]{:S(2)}) %collective-permute-start.23) | collective-permute-done | bytes 344096 | tf_op jit(solution)/shard_map/ppermute | solution.py:24
  213.7 2.6 collective-permute-done.25
  223.0 9.4 %collective-permute-done.27 = bf16[64,3584]{1,0:T(8,128)(2,1)S(1)} collective-permute-done((bf16[64,3584]{1,0:T(8,128)(2,1)S(1)}, bf16[64,3584]{1,0:T(8,128)(2,1)S(1)}, u32[]{:S(2)}, u32[]{:S(2)}) %collective-permute-start.27) | collective-permute-done | bytes 458784 | tf_op jit(solution)/shard_map/ppermute | solution.py:24
  244.0 4.6 %fusion.7 = bf16[1,1,3584,512]{3,2,1,0:T(8,128)(2,1)} fusion(bf16[768,3584]{1,0:T(8,128)(2,1)S(1)} %constant_dynamic-update-slice_fusion.85, bf16[768,512]{1,0:T(8,128)(2,1)S(1)} %constant_dynamic-update-slice_fusion.89), kind=kOutput, calls=%fused_computation.10 | convolution fusion | flops 2820407296 | bytes 9961472 | tf_op jit(solution)/shard_map/dot_general | solution.py:80
  248.6 6.2 %collective-permute-done.30 = bf16[2,2,24,3584]{3,2,0,1:T(8,128)(2,1)S(1)} collective-permute-done((bf16[2,2,24,3584]{3,2,0,1:T(8,128)(2,1)S(1)}, bf16[2,2,24,3584]{3,2,0,1:T(8,128)(2,1)S(1)}, u32[]{:S(2)}, u32[]{:S(2)}) %collective-permute-start.30) | collective-permute-done | bytes 688160 | tf_op jit(solution)/shard_map/ppermute | solution.py:24
  255.2 3.8 %collective-permute-done.35 = bf16[128,3584]{1,0:T(8,128)(2,1)S(1)} collective-permute-done((bf16[128,3584]{1,0:T(8,128)(2,1)S(1)}, bf16[128,3584]{1,0:T(8,128)(2,1)S(1)}, u32[]{:S(2)}, u32[]{:S(2)}) %collective-permute-start.35) | collective-permute-done | bytes 917536 | tf_op jit(solution)/shard_map/ppermute | solution.py:24
  259.0 3.3 %collective-permute-done.34 = bf16[128,3584]{1,0:T(8,128)(2,1)S(1)} collective-permute-done((bf16[128,3584]{1,0:T(8,128)(2,1)S(1)}, bf16[128,3584]{1,0:T(8,128)(2,1)S(1)}, u32[]{:S(2)}, u32[]{:S(2)}) %collective-permute-start.34) | collective-permute-done | bytes 917536 | tf_op jit(solution)/shard_map/ppermute | solution.py:24
  263.0 3.0 %collective-permute-start.36 = (bf16[128,3584]{1,0:T(8,128)(2,1)S(1)}, bf16[128,3584]{1,0:T(8,128)(2,1)S(1)}, u32[]{:S(2)}, u32[]{:S(2)}) collective-permute-start(bf16[128,3584]{1,0:T(8,128)(2,1)S(1)} %add_convert_fusion.2), channel_id=1, source_target_pairs={{32,0},{64,32},{96,64},{33,1},{65,33},{97,65},{34,2},{66,34},{98,6... | collective-permute-start | bytes 2752520 | tf_op jit(solution)/shard_map/ppermute | solution.py:46
  269.0 4.6 %fusion.8 = bf16[1,1,3584,512]{3,2,1,0:T(8,128)(2,1)} fusion(bf16[768,3584]{1,0:T(8,128)(2,1)S(1)} %constant_dynamic-update-slice_fusion.85, bf16[768,512]{1,0:T(8,128)(2,1)S(1)} %constant_dynamic-update-slice_fusion.105), kind=kOutput, calls=%fused_computation.11 | convolution fusion | flops 2820407296 | bytes 9961472 | tf_op jit(solution)/shard_map/dot_general | solution.py:80
  273.6 11.6 %collective-permute-done.36 = bf16[128,3584]{1,0:T(8,128)(2,1)S(1)} collective-permute-done((bf16[128,3584]{1,0:T(8,128)(2,1)S(1)}, bf16[128,3584]{1,0:T(8,128)(2,1)S(1)}, u32[]{:S(2)}, u32[]{:S(2)}) %collective-permute-start.36) | collective-permute-done | bytes 917536 | tf_op jit(solution)/shard_map/ppermute | solution.py:46
  285.2 6.1 %collective-permute-done.33 = bf16[128,3584]{1,0:T(8,128)(2,1)S(1)} collective-permute-done((bf16[128,3584]{1,0:T(8,128)(2,1)S(1)}, bf16[128,3584]{1,0:T(8,128)(2,1)S(1)}, u32[]{:S(2)}, u32[]{:S(2)}) %collective-permute-start.33) | collective-permute-done | bytes 917536 | tf_op jit(solution)/shard_map/ppermute | solution.py:46
  (432 shorter events, 98.1 us)
Async XLA Ops:
  6.4 25.3 %collective-permute-start.2 = (bf16[136,3584]{1,0:T(8,128)(2,1)}, bf16[136,3584]{1,0:T(8,128)(2,1)}, u32[]{:S(2)}, u32[]{:S(2)}) collective-permute-start(bf16[136,3584]{1,0:T(8,128)(2,1)} %fusion.19), channel_id=1, source_target_pairs={{0,5},{2,7},{4,0},{6,2},{1,4},{3,6},{5,1},{7,3},{8,13},{10,15},{12... | collective-permute-start | bytes 2924552 | tf_op jit(solution)/shard_map/ppermute | solution.py:24
  10.5 24.6 %collective-permute-start.1 = (bf16[136,3584]{1,0:T(8,128)(2,1)}, bf16[136,3584]{1,0:T(8,128)(2,1)}, u32[]{:S(2)}, u32[]{:S(2)}) collective-permute-start(bf16[136,3584]{1,0:T(8,128)(2,1)} %fusion.19), channel_id=1, source_target_pairs={{0,4},{2,6},{4,1},{6,3},{1,5},{3,7},{5,0},{7,2},{8,12},{10,14},{12... | collective-permute-start | bytes 2924552 | tf_op jit(solution)/shard_map/ppermute | solution.py:24
  15.3 19.8 %collective-permute-start.3 = (bf16[96,3584]{1,0:T(8,128)(2,1)S(1)}, bf16[96,3584]{1,0:T(8,128)(2,1)S(1)}, u32[]{:S(2)}, u32[]{:S(2)}) collective-permute-start(bf16[96,3584]{1,0:T(8,128)(2,1)S(1)} %pad_maximum_fusion.4), channel_id=1, source_target_pairs={{0,8},{2,10},{4,12},{6,14},{1,9},{3,11},{5,13},{7,15},{8,16},{10,1... | collective-permute-start | bytes 2064392 | tf_op jit(solution)/shard_map/ppermute | solution.py:24
  17.0 18.1 %collective-permute-start.4 = (bf16[96,3584]{1,0:T(8,128)(2,1)S(1)}, bf16[96,3584]{1,0:T(8,128)(2,1)S(1)}, u32[]{:S(2)}, u32[]{:S(2)}) collective-permute-start(bf16[96,3584]{1,0:T(8,128)(2,1)S(1)} %pad_maximum_fusion.5), channel_id=1, source_target_pairs={{0,24},{2,26},{4,28},{6,30},{1,25},{3,27},{5,29},{7,31},{8,0},{10,... | collective-permute-start | bytes 2064392 | tf_op jit(solution)/shard_map/ppermute | solution.py:24
  39.2 12.9 %collective-permute-start.5 = (bf16[64,3584]{1,0:T(8,128)(2,1)S(1)}, bf16[64,3584]{1,0:T(8,128)(2,1)S(1)}, u32[]{:S(2)}, u32[]{:S(2)}) collective-permute-start(bf16[64,3584]{1,0:T(8,128)(2,1)S(1)} %slice.820), channel_id=1, source_target_pairs={{0,4},{2,6},{4,1},{6,3},{1,5},{3,7},{5,0},{7,2},{8,12},{10,14},{12... | collective-permute-start | bytes 1376264 | tf_op jit(solution)/shard_map/ppermute | solution.py:24
  39.2 12.9 %collective-permute-start.6 = (bf16[72,3584]{1,0:T(8,128)(2,1)S(1)}, bf16[72,3584]{1,0:T(8,128)(2,1)S(1)}, u32[]{:S(2)}, u32[]{:S(2)}) collective-permute-start(bf16[72,3584]{1,0:T(8,128)(2,1)S(1)} %slice.821), channel_id=1, source_target_pairs={{0,5},{2,7},{4,0},{6,2},{1,4},{3,6},{5,1},{7,3},{8,13},{10,15},{12... | collective-permute-start | bytes 1548296 | tf_op jit(solution)/shard_map/ppermute | solution.py:24
  42.5 17.1 %collective-permute-start.7 = (bf16[96,3584]{1,0:T(8,128)(2,1)S(1)}, bf16[96,3584]{1,0:T(8,128)(2,1)S(1)}, u32[]{:S(2)}, u32[]{:S(2)}) collective-permute-start(bf16[96,3584]{1,0:T(8,128)(2,1)S(1)} %pad_maximum_fusion.6), channel_id=1, source_target_pairs={{0,16},{2,18},{4,20},{6,22},{1,17},{3,19},{5,21},{7,23},{8,24},{10... | collective-permute-start | bytes 2064392 | tf_op jit(solution)/shard_map/ppermute | solution.py:24
  59.8 29.4 %collective-permute-start.9 = (bf16[192,3584]{1,0:T(8,128)(2,1)S(1)}, bf16[192,3584]{1,0:T(8,128)(2,1)S(1)}, u32[]{:S(2)}, u32[]{:S(2)}) collective-permute-start(bf16[192,3584]{1,0:T(8,128)(2,1)S(1)} %get-tuple-element.366), channel_id=1, source_target_pairs={{0,5},{2,7},{4,0},{6,2},{1,4},{3,6},{5,1},{7,3},{8,13},{10,15},{12... | collective-permute-start | bytes 4128776 | tf_op jit(solution)/shard_map/ppermute | solution.py:24
  62.0 30.5 %collective-permute-start.8 = (bf16[192,3584]{1,0:T(8,128)(2,1)S(1)}, bf16[192,3584]{1,0:T(8,128)(2,1)S(1)}, u32[]{:S(2)}, u32[]{:S(2)}) collective-permute-start(bf16[192,3584]{1,0:T(8,128)(2,1)S(1)} %get-tuple-element.366), channel_id=1, source_target_pairs={{0,4},{2,6},{4,1},{6,3},{1,5},{3,7},{5,0},{7,2},{8,12},{10,14},{12... | collective-permute-start | bytes 4128776 | tf_op jit(solution)/shard_map/ppermute | solution.py:24
  65.4 33.4 %collective-permute-start.11 = (bf16[192,3584]{1,0:T(8,128)(2,1)S(1)}, bf16[192,3584]{1,0:T(8,128)(2,1)S(1)}, u32[]{:S(2)}, u32[]{:S(2)}) collective-permute-start(bf16[192,3584]{1,0:T(8,128)(2,1)S(1)} %bitcast.356), channel_id=1, source_target_pairs={{0,8},{2,10},{4,12},{6,14},{1,9},{3,11},{5,13},{7,15},{8,16},{10,1... | collective-permute-start | bytes 4128776 | tf_op jit(solution)/shard_map/ppermute | solution.py:24
  67.0 31.8 %collective-permute-start.12 = (bf16[192,3584]{1,0:T(8,128)(2,1)S(1)}, bf16[192,3584]{1,0:T(8,128)(2,1)S(1)}, u32[]{:S(2)}, u32[]{:S(2)}) collective-permute-start(bf16[192,3584]{1,0:T(8,128)(2,1)S(1)} %bitcast.355), channel_id=1, source_target_pairs={{0,24},{2,26},{4,28},{6,30},{1,25},{3,27},{5,29},{7,31},{8,0},{10,... | collective-permute-start | bytes 4128776 | tf_op jit(solution)/shard_map/ppermute | solution.py:24
  99.9 36.2 %collective-permute-start.15 = (bf16[192,3584]{1,0:T(8,128)(2,1)}, bf16[192,3584]{1,0:T(8,128)(2,1)}, u32[]{:S(2)}, u32[]{:S(2)}) collective-permute-start(bf16[192,3584]{1,0:T(8,128)(2,1)} %bitcast.61), channel_id=1, source_target_pairs={{0,16},{2,18},{4,20},{6,22},{1,17},{3,19},{5,21},{7,23},{8,24},{10... | collective-permute-start | bytes 4128776 | tf_op jit(solution)/shard_map/ppermute | solution.py:24
  102.8 33.3 %collective-permute-start.14 = (bf16[192,3584]{1,0:T(8,128)(2,1)S(1)}, bf16[192,3584]{1,0:T(8,128)(2,1)}, u32[]{:S(2)}, u32[]{:S(2)}) collective-permute-start(bf16[192,3584]{1,0:T(8,128)(2,1)S(1)} %get-tuple-element.224.refs_2_), channel_id=1, source_target_pairs={{0,1},{2,3},{4,5},{6,7},{1,0},{3,2},{5,4},{7,6},{8,9},{10,11},{12,... | collective-permute-start | bytes 4128776 | tf_op jit(solution)/shard_map/ppermute | solution.py:24
  136.1 31.3 %collective-permute-start.16 = (bf16[192,3584]{1,0:T(8,128)(2,1)}, bf16[192,3584]{1,0:T(8,128)(2,1)}, u32[]{:S(2)}, u32[]{:S(2)}) collective-permute-start(bf16[192,3584]{1,0:T(8,128)(2,1)} %get-tuple-element.178), channel_id=1, source_target_pairs={{0,5},{2,7},{4,0},{6,2},{1,4},{3,6},{5,1},{7,3},{8,13},{10,15},{12... | collective-permute-start | bytes 4128776 | tf_op jit(solution)/shard_map/ppermute | solution.py:24
  138.3 31.3 %collective-permute-start.17 = (bf16[192,3584]{1,0:T(8,128)(2,1)}, bf16[192,3584]{1,0:T(8,128)(2,1)}, u32[]{:S(2)}, u32[]{:S(2)}) collective-permute-start(bf16[192,3584]{1,0:T(8,128)(2,1)} %get-tuple-element.179), channel_id=1, source_target_pairs={{0,4},{2,6},{4,1},{6,3},{1,5},{3,7},{5,0},{7,2},{8,12},{10,14},{12... | collective-permute-start | bytes 4128776 | tf_op jit(solution)/shard_map/ppermute | solution.py:24
  138.5 23.1 %collective-permute-start.18 = (bf16[144,3584]{1,0:T(8,128)(2,1)S(1)}, bf16[144,3584]{1,0:T(8,128)(2,1)}, u32[]{:S(2)}, u32[]{:S(2)}) collective-permute-start(bf16[144,3584]{1,0:T(8,128)(2,1)S(1)} %get-tuple-element.180), channel_id=1, source_target_pairs={{0,24},{2,26},{4,28},{6,30},{1,25},{3,27},{5,29},{7,31},{8,0},{10,... | collective-permute-start | bytes 3096584 | tf_op jit(solution)/shard_map/ppermute | solution.py:24
  139.9 23.9 %collective-permute-start.19 = (bf16[144,3584]{1,0:T(8,128)(2,1)}, bf16[144,3584]{1,0:T(8,128)(2,1)}, u32[]{:S(2)}, u32[]{:S(2)}) collective-permute-start(bf16[144,3584]{1,0:T(8,128)(2,1)} %get-tuple-element.181), channel_id=1, source_target_pairs={{0,8},{2,10},{4,12},{6,14},{1,9},{3,11},{5,13},{7,15},{8,16},{10,1... | collective-permute-start | bytes 3096584 | tf_op jit(solution)/shard_map/ppermute | solution.py:24
  169.7 13.6 %collective-permute-start.22 = (bf16[48,3584]{1,0:T(8,128)(2,1)S(1)}, bf16[48,3584]{1,0:T(8,128)(2,1)S(1)}, u32[]{:S(2)}, u32[]{:S(2)}) collective-permute-start(bf16[48,3584]{1,0:T(8,128)(2,1)S(1)} %get-tuple-element.200), channel_id=1, source_target_pairs={{0,24},{2,26},{4,28},{6,30},{1,25},{3,27},{5,29},{7,31},{8,0},{10,... | collective-permute-start | bytes 1032200 | tf_op jit(solution)/shard_map/ppermute | solution.py:24
  171.1 38.0 %collective-permute-start.23 = (bf16[48,3584]{1,0:T(8,128)(2,1)S(1)}, bf16[48,3584]{1,0:T(8,128)(2,1)S(1)}, u32[]{:S(2)}, u32[]{:S(2)}) collective-permute-start(bf16[48,3584]{1,0:T(8,128)(2,1)S(1)} %get-tuple-element.201), channel_id=1, source_target_pairs={{0,8},{2,10},{4,12},{6,14},{1,9},{3,11},{5,13},{7,15},{8,16},{10,1... | collective-permute-start | bytes 1032200 | tf_op jit(solution)/shard_map/ppermute | solution.py:24
  171.8 37.3 %collective-permute-start.24 = (bf16[96,3584]{1,0:T(8,128)(2,1)S(1)}, bf16[96,3584]{1,0:T(8,128)(2,1)S(1)}, u32[]{:S(2)}, u32[]{:S(2)}) collective-permute-start(bf16[96,3584]{1,0:T(8,128)(2,1)S(1)} %slice.905), channel_id=1, source_target_pairs={{0,2},{2,0},{4,6},{6,4},{1,3},{3,1},{5,7},{7,5},{8,10},{10,8},{12,... | collective-permute-start | bytes 2064392 | tf_op jit(solution)/shard_map/ppermute | solution.py:24
  171.8 37.3 %collective-permute-start.20 = (bf16[192,3584]{1,0:T(8,128)(2,1)S(1)}, bf16[192,3584]{1,0:T(8,128)(2,1)S(1)}, u32[]{:S(2)}, u32[]{:S(2)}) collective-permute-start(bf16[192,3584]{1,0:T(8,128)(2,1)S(1)} %get-tuple-element.197), channel_id=1, source_target_pairs={{0,1},{2,3},{4,5},{6,7},{1,0},{3,2},{5,4},{7,6},{8,9},{10,11},{12,... | collective-permute-start | bytes 4128776 | tf_op jit(solution)/shard_map/ppermute | solution.py:24
  173.2 35.9 %collective-permute-start.21 = (bf16[192,3584]{1,0:T(8,128)(2,1)S(1)}, bf16[192,3584]{1,0:T(8,128)(2,1)S(1)}, u32[]{:S(2)}, u32[]{:S(2)}) collective-permute-start(bf16[192,3584]{1,0:T(8,128)(2,1)S(1)} %get-tuple-element.199), channel_id=1, source_target_pairs={{0,16},{2,18},{4,20},{6,22},{1,17},{3,19},{5,21},{7,23},{8,24},{10... | collective-permute-start | bytes 4128776 | tf_op jit(solution)/shard_map/ppermute | solution.py:24
  217.6 17.6 %collective-permute-start.28 = (bf16[2,2,24,3584]{3,2,0,1:T(8,128)(2,1)S(1)}, bf16[2,2,24,3584]{3,2,0,1:T(8,128)(2,1)S(1)}, u32[]{:S(2)}, u32[]{:S(2)}) collective-permute-start(bf16[2,2,24,3584]{3,2,0,1:T(8,128)(2,1)S(1)} %pad_maximum_fusion.8), channel_id=1, source_target_pairs={{0,24},{2,26},{4,28},{6,30},{1,25},{3,27},{5,29},{7,31},{8,0},{10,... | collective-permute-start | bytes 2064392 | tf_op jit(solution)/shard_map/ppermute | solution.py:24
  218.2 18.4 %collective-permute-start.29 = (bf16[2,2,24,3584]{3,2,1,0:T(8,128)(2,1)S(1)}, bf16[2,2,24,3584]{3,2,1,0:T(8,128)(2,1)S(1)}, u32[]{:S(2)}, u32[]{:S(2)}) collective-permute-start(bf16[2,2,24,3584]{3,2,1,0:T(8,128)(2,1)S(1)} %pad_maximum_fusion.10), channel_id=1, source_target_pairs={{0,8},{2,10},{4,12},{6,14},{1,9},{3,11},{5,13},{7,15},{8,16},{10,1... | collective-permute-start | bytes 2064392 | tf_op jit(solution)/shard_map/ppermute | solution.py:24
  220.3 12.1 %collective-permute-start.27 = (bf16[64,3584]{1,0:T(8,128)(2,1)S(1)}, bf16[64,3584]{1,0:T(8,128)(2,1)S(1)}, u32[]{:S(2)}, u32[]{:S(2)}) collective-permute-start(bf16[64,3584]{1,0:T(8,128)(2,1)S(1)} %get-tuple-element.359), channel_id=1, source_target_pairs={{0,5},{2,7},{4,0},{6,2},{1,4},{3,6},{5,1},{7,3},{8,13},{10,15},{12... | collective-permute-start | bytes 1376264 | tf_op jit(solution)/shard_map/ppermute | solution.py:24
  220.7 13.0 %collective-permute-start.26 = (bf16[64,3584]{1,0:T(8,128)(2,1)S(1)}, bf16[64,3584]{1,0:T(8,128)(2,1)S(1)}, u32[]{:S(2)}, u32[]{:S(2)}) collective-permute-start(bf16[64,3584]{1,0:T(8,128)(2,1)S(1)} %get-tuple-element.360), channel_id=1, source_target_pairs={{0,4},{2,6},{4,1},{6,3},{1,5},{3,7},{5,0},{7,2},{8,12},{10,14},{12... | collective-permute-start | bytes 1376264 | tf_op jit(solution)/shard_map/ppermute | solution.py:24
  236.8 17.9 %collective-permute-start.30 = (bf16[2,2,24,3584]{3,2,0,1:T(8,128)(2,1)S(1)}, bf16[2,2,24,3584]{3,2,0,1:T(8,128)(2,1)S(1)}, u32[]{:S(2)}, u32[]{:S(2)}) collective-permute-start(bf16[2,2,24,3584]{3,2,0,1:T(8,128)(2,1)S(1)} %pad_maximum_fusion.9), channel_id=1, source_target_pairs={{0,16},{2,18},{4,20},{6,22},{1,17},{3,19},{5,21},{7,23},{8,24},{10... | collective-permute-start | bytes 2064392 | tf_op jit(solution)/shard_map/ppermute | solution.py:24
  237.6 21.4 %collective-permute-start.35 = (bf16[128,3584]{1,0:T(8,128)(2,1)S(1)}, bf16[128,3584]{1,0:T(8,128)(2,1)S(1)}, u32[]{:S(2)}, u32[]{:S(2)}) collective-permute-start(bf16[128,3584]{1,0:T(8,128)(2,1)S(1)} %pad_maximum_fusion.2), channel_id=1, source_target_pairs={{0,5},{2,7},{4,0},{6,2},{1,4},{3,6},{5,1},{7,3},{8,13},{10,15},{12... | collective-permute-start | bytes 2752520 | tf_op jit(solution)/shard_map/ppermute | solution.py:24
  238.2 27.9 %collective-permute-start.31 = (bf16[3,2,24,3584]{3,2,1,0:T(8,128)(2,1)S(1)}, bf16[3,2,24,3584]{3,2,1,0:T(8,128)(2,1)S(1)}, u32[]{:S(2)}, u32[]{:S(2)}) collective-permute-start(bf16[3,2,24,3584]{3,2,1,0:T(8,128)(2,1)S(1)} %pad_maximum_fusion), channel_id=1, source_target_pairs={{0,2},{2,0},{4,6},{6,4},{1,3},{3,1},{5,7},{7,5},{8,10},{10,8},{12,... | collective-permute-start | bytes 3096584 | tf_op jit(solution)/shard_map/ppermute | solution.py:24
  238.3 24.0 %collective-permute-start.34 = (bf16[128,3584]{1,0:T(8,128)(2,1)S(1)}, bf16[128,3584]{1,0:T(8,128)(2,1)S(1)}, u32[]{:S(2)}, u32[]{:S(2)}) collective-permute-start(bf16[128,3584]{1,0:T(8,128)(2,1)S(1)} %pad_maximum_fusion.1), channel_id=1, source_target_pairs={{0,4},{2,6},{4,1},{6,3},{1,5},{3,7},{5,0},{7,2},{8,12},{10,14},{12... | collective-permute-start | bytes 2752520 | tf_op jit(solution)/shard_map/ppermute | solution.py:24
  263.0 22.2 %collective-permute-start.36 = (bf16[128,3584]{1,0:T(8,128)(2,1)S(1)}, bf16[128,3584]{1,0:T(8,128)(2,1)S(1)}, u32[]{:S(2)}, u32[]{:S(2)}) collective-permute-start(bf16[128,3584]{1,0:T(8,128)(2,1)S(1)} %add_convert_fusion.2), channel_id=1, source_target_pairs={{32,0},{64,32},{96,64},{33,1},{65,33},{97,65},{34,2},{66,34},{98,6... | collective-permute-start | bytes 2752520 | tf_op jit(solution)/shard_map/ppermute | solution.py:46
  267.7 23.6 %collective-permute-start.33 = (bf16[128,3584]{1,0:T(8,128)(2,1)S(1)}, bf16[128,3584]{1,0:T(8,128)(2,1)S(1)}, u32[]{:S(2)}, u32[]{:S(2)}) collective-permute-start(bf16[128,3584]{1,0:T(8,128)(2,1)S(1)} %fusion.17), channel_id=1, source_target_pairs={{0,32},{32,64},{64,96},{1,33},{33,65},{65,97},{2,34},{34,66},{66,9... | collective-permute-start | bytes 2752520 | tf_op jit(solution)/shard_map/ppermute | solution.py:46
  (100 other events, 657.7 us)

commit v2 on v0

--- a/solution.py
+++ b/solution.py
@@ -302,7 +302,8 @@
         for dl in range(2)
     ]
     x1, x3 = shift_z(other, 1), shift_z(other, 3)
-    odd, even = swap_core(cross[0]), swap_core(cross[1])
+    odd, cross_even = lax.optimization_barrier((swap_core(cross[0]), cross[1]))
+    even = swap_core(cross_even)
     sib = [even[:4], odd[:4], even[4:], odd[4:]]
     out_y = [
         jnp.concatenate([jnp.stack([sel[s][0, t] for s in range(4)]), sib[t]]).reshape(flat, width)

time: 288 us -> 286 us (level)
  transfers between devices with their start and end apart: 37 -> 37, of which waited for: 20 -> 20; matrix products, arithmetic and copies ran while one was open for 15% -> 16% of each run, Pallas kernels for 13% -> 13%
where the time goes in v2:
time: 286 us; the launch traced here: 285 us
  waiting for transfers between devices  131 us (46%)
  starting transfers between devices  49.9 us (17%)
  Pallas kernels  36.1 us (13%)
  local copies, waits for them, and re-layouts  30.4 us (11%)
  matrix products  26.2 us (9%)
  other arithmetic  8.52 us (3%)
    ppermute x35, waiting for transfers between devices, shifted(): return lax.ppermute(x, GROUP, pairs)  115 us
    ppermute x35, starting transfers between devices, shifted(): return lax.ppermute(x, GROUP, pairs)  45.6 us
    dot_general x9, matrix products, mm_first(): lax.dot_general(a, b, (((0,), (0,)), ((), ())), preferred_element_type=F32)  21.7 us
    unnamed x219, local copies, waits for them, and re-layouts  20.7 us
    ppermute x2, waiting for transfers between devices, from_behind(): return lax.ppermute(x, axis, pairs)  16.1 us
    pallas_call x2, Pallas kernels, backward(): kernel_call(body, 7, [whole(a) for a in operands] + [rows_block(n, units)...  12.8 us
    pallas_call x2, Pallas kernels, forward(): kernel_call(body, 2, [whole(x) for x in pieces] + [columns(depth, n)] * 2...  8.99 us
    pallas_call x2, Pallas kernels, outputs(): kernel_call(body, 7, [whole(h) for h in hidden] + [columns(units, n)], [c...  7.49 us
  transfers between devices with their start and end apart: 37, of which 20 were waited for; matrix products, arithmetic and copies ran while one was open for 16% of the time, Pallas kernels for 13%

profile of v2, /device:TPU:6, one launch (start us, length us, event | category | flops | bytes accessed | tf_op | source)
XLA Modules:
  0.0 284.7 jit_solution(651775070703066196)
XLA Ops:
  17.0 15.4 %collective-permute-done.1 = bf16[136,3584]{1,0:T(8,128)(2,1)} collective-permute-done((bf16[136,3584]{1,0:T(8,128)(2,1)}, bf16[136,3584]{1,0:T(8,128)(2,1)}, u32[]{:S(2)}, u32[]{:S(2)}) %collective-permute-start.1) | collective-permute-done | bytes 974880 | tf_op jit(solution)/shard_map/ppermute | solution.py:24
  34.2 3.0 %collective-permute-start.6 = (bf16[72,3584]{1,0:T(8,128)(2,1)S(1)}, bf16[72,3584]{1,0:T(8,128)(2,1)S(1)}, u32[]{:S(2)}, u32[]{:S(2)}) collective-permute-start(bf16[72,3584]{1,0:T(8,128)(2,1)S(1)} %slice.821), channel_id=1, source_target_pairs={{0,5},{2,7},{4,0},{6,2},{1,4},{3,6},{5,1},{7,3},{8,13},{10,15},{12... | collective-permute-start | bytes 1548296 | tf_op jit(solution)/shard_map/ppermute | solution.py:24
  39.6 3.3 %collective-permute-start.7 = (bf16[96,3584]{1,0:T(8,128)(2,1)S(1)}, bf16[96,3584]{1,0:T(8,128)(2,1)S(1)}, u32[]{:S(2)}, u32[]{:S(2)}) collective-permute-start(bf16[96,3584]{1,0:T(8,128)(2,1)S(1)} %pad_maximum_fusion.6), channel_id=1, source_target_pairs={{0,16},{2,18},{4,20},{6,22},{1,17},{3,19},{5,21},{7,23},{8,24},{10... | collective-permute-start | bytes 2064392 | tf_op jit(solution)/shard_map/ppermute | solution.py:24
  42.9 5.2 %collective-permute-done.6 = bf16[72,3584]{1,0:T(8,128)(2,1)S(1)} collective-permute-done((bf16[72,3584]{1,0:T(8,128)(2,1)S(1)}, bf16[72,3584]{1,0:T(8,128)(2,1)S(1)}, u32[]{:S(2)}, u32[]{:S(2)}) %collective-permute-start.6) | collective-permute-done | bytes 516128 | tf_op jit(solution)/shard_map/ppermute | solution.py:24
  48.4 4.3 %collective-permute-done.5 = bf16[64,3584]{1,0:T(8,128)(2,1)S(1)} collective-permute-done((bf16[64,3584]{1,0:T(8,128)(2,1)S(1)}, bf16[64,3584]{1,0:T(8,128)(2,1)S(1)}, u32[]{:S(2)}, u32[]{:S(2)}) %collective-permute-start.5) | collective-permute-done | bytes 458784 | tf_op jit(solution)/shard_map/ppermute | solution.py:24
  58.5 3.2 %collective-permute-start.9 = (bf16[192,3584]{1,0:T(8,128)(2,1)S(1)}, bf16[192,3584]{1,0:T(8,128)(2,1)S(1)}, u32[]{:S(2)}, u32[]{:S(2)}) collective-permute-start(bf16[192,3584]{1,0:T(8,128)(2,1)S(1)} %get-tuple-element.360), channel_id=1, source_target_pairs={{0,5},{2,7},{4,0},{6,2},{1,4},{3,6},{5,1},{7,3},{8,13},{10,15},{12... | collective-permute-start | bytes 4128776 | tf_op jit(solution)/shard_map/ppermute | solution.py:24
  69.5 20.9 %collective-permute-done.8.refs_0_ = bf16[192,3584]{1,0:T(8,128)(2,1)S(1)} collective-permute-done((bf16[192,3584]{1,0:T(8,128)(2,1)S(1)}, bf16[192,3584]{1,0:T(8,128)(2,1)S(1)}, u32[]{:S(2)}, u32[]{:S(2)}) %collective-permute-start.8) | collective-permute-done | bytes 1376288 | tf_op jit(solution)/shard_map/ppermute | solution.py:24
  90.4 8.6 %collective-permute-done.11.refs_0_ = bf16[192,3584]{1,0:T(8,128)(2,1)S(1)} collective-permute-done((bf16[192,3584]{1,0:T(8,128)(2,1)S(1)}, bf16[192,3584]{1,0:T(8,128)(2,1)S(1)}, u32[]{:S(2)}, u32[]{:S(2)}) %collective-permute-start.11) | collective-permute-done | bytes 1376288 | tf_op jit(solution)/shard_map/ppermute | solution.py:24
  101.0 2.9 %collective-permute-start.15 = (bf16[192,3584]{1,0:T(8,128)(2,1)}, bf16[192,3584]{1,0:T(8,128)(2,1)}, u32[]{:S(2)}, u32[]{:S(2)}) collective-permute-start(bf16[192,3584]{1,0:T(8,128)(2,1)} %bitcast.61), channel_id=1, source_target_pairs={{0,16},{2,18},{4,20},{6,22},{1,17},{3,19},{5,21},{7,23},{8,24},{10... | collective-permute-start | bytes 4128776 | tf_op jit(solution)/shard_map/ppermute | solution.py:24
  103.8 5.4 %shard_map.110 = (f32[192,512]{1,0:T(8,128)S(1)}, f32[192,512]{1,0:T(8,128)S(1)}, bf16[192,512]{1,0:T(8,128)(2,1)S(1)}, f32[192,512]{1,0:T(8,128)S(1)}, f32[192,...) custom-call(bf16[192,3584]{1,0:T(8,128)(2,1)S(1)} %collective-permut, ...), custom_call_target="tpu_custom_call" | custom-call | flops 1 | bytes 1 | tf_op jit(solution)/shard_map/pallas_call | solution.py:123
  110.8 4.4 %shard_map.111 = (bf16[192,3584]{1,0:T(8,128)(2,1)}, bf16[192,3584]{1,0:T(8,128)(2,1)}) custom-call(bf16[192,512]{1,0:T(8,128)(2,1)S(1)} %get-tuple-element.258.refs_0_, bf16[192,512]{1,0:T(8,128)(2,1)S(1)} %get-tuple-element.260.refs_1_, bf16[512,3584]{1,0:T(8,128)(2,1)S(1)} %bitcast.308), custom_call_target="tpu_custom_call" | custom-call | flops 1 | bytes 1 | tf_op jit(solution)/shard_map/pallas_call | solution.py:142
  119.2 3.9 %shard_map.112 = (f32[192,512]{1,0:T(8,128)S(1)}, f32[192,512]{1,0:T(8,128)S(1)}, f32[192,512]{1,0:T(8,128)S(1)}) custom-call(bf16[192,3584]{1,0:T(8,128)(2,1)S(1)} %copy-done.23, bf16[192,3584]{1,0:T(8,128)(2,1)S(1)} %copy-done.26, bf16[192,3584]{1,0:T(8,128)(2,1)S(1)} %bitcast.312, bf16[512,3584]{1,0:T(8,128)(2,1)S(1)} %bitcast.309), custom_call_target="tpu_custom_call" | custom-call | flops 1 | bytes 1 | tf_op jit(solution)/shard_map/pallas_call | solution.py:160
  123.3 5.1 %shard_map.113 = (bf16[144,3584]{1,0:T(8,128)(2,1)}, bf16[144,3584]{1,0:T(8,128)(2,1)}, bf16[288,512]{1,0:T(8,128)(2,1)S(1)}, bf16[288,512]{1,0:T(8,128)(2,1)S(1)}) custom-call(f32[192,512]{1,0:T(8,128)S(1)} %copy-done.19, f32[192,512]{1,0:T(8,128)S(1)} %get-tuple-element.166.refs_1_, f32[192,512]{1,0:T(8,128)S(1)} %copy-done.15, f32[192,512]{1,0:T(8,128)S(1)} %copy-done.21, ...), custom_call_target="tpu_custom_call" | custom-call | flops 1 | bytes 1 | tf_op jit(solution)/shard_map/pallas_call | solution.py:214
  128.4 5.0 %collective-permute-done.14.refs_0_ = bf16[192,3584]{1,0:T(8,128)(2,1)} collective-permute-done((bf16[192,3584]{1,0:T(8,128)(2,1)S(1)}, bf16[192,3584]{1,0:T(8,128)(2,1)}, u32[]{:S(2)}, u32[]{:S(2)}) %collective-permute-start.14) | collective-permute-done | bytes 1376288 | tf_op jit(solution)/shard_map/ppermute | solution.py:24
  140.9 3.6 %shard_map.114 = (f32[192,512]{1,0:T(8,128)S(1)}, f32[192,512]{1,0:T(8,128)S(1)}, bf16[192,512]{1,0:T(8,128)(2,1)S(1)}) custom-call(bf16[192,3584]{1,0:T(8,128)(2,1)} %collective-permute-done.14.refs_0_, bf16[3584,512]{1,0:T(8,128)(2,1)S(1)} %bitcast.302, bf16[3584,512]{1,0:T(8,128)(2,1)S(1)} %bitcast.307), custom_call_target="tpu_custom_call" | custom-call | flops 1 | bytes 1 | tf_op jit(solution)/shard_map/pallas_call | solution.py:123
  145.3 2.9 %shard_map.116.refs_9_ = f32[192,512]{1,0:T(8,128)S(1)} custom-call(bf16[192,3584]{1,0:T(8,128)(2,1)} %collective-permute-done.15.refs_0_, bf16[512,3584]{1,0:T(8,128)(2,1)S(1)} %bitcast.310), custom_call_target="tpu_custom_call" | custom-call | flops 1 | bytes 1 | tf_op jit(solution)/shard_map/pallas_call | solution.py:160
  148.2 3.1 %shard_map.115 = (bf16[192,3584]{1,0:T(8,128)(2,1)S(1)}, bf16[192,3584]{1,0:T(8,128)(2,1)S(1)}) custom-call(bf16[192,512]{1,0:T(8,128)(2,1)S(1)} %get-tuple-element.259.refs_0_, bf16[192,512]{1,0:T(8,128)(2,1)S(1)} %get-tuple-element.257.refs_1_, bf16[512,3584]{1,0:T(8,128)(2,1)S(1)} %bitcast.311), custom_call_target="tpu_custom_call" | custom-call | flops 1 | bytes 1 | tf_op jit(solution)/shard_map/pallas_call | solution.py:142
  151.3 7.6 %shard_map.117 = (bf16[192,3584]{1,0:T(8,128)(2,1)S(1)}, bf16[192,3584]{1,0:T(8,128)(2,1)S(1)}, bf16[48,3584]{1,0:T(8,128)(2,1)S(1)}, bf16[48,3584]{1,0:T(8,128)...) custom-call(f32[192,512]{1,0:T(8,128)S(1)} %copy-done.19, ...), custom_call_target="tpu_custom_call" | custom-call | flops 1 | bytes 1 | tf_op jit(solution)/shard_map/pallas_call | solution.py:214
  159.1 3.4 %collective-permute-done.19 = bf16[144,3584]{1,0:T(8,128)(2,1)} collective-permute-done((bf16[144,3584]{1,0:T(8,128)(2,1)}, bf16[144,3584]{1,0:T(8,128)(2,1)}, u32[]{:S(2)}, u32[]{:S(2)}) %collective-permute-start.19) | collective-permute-done | bytes 1032224 | tf_op jit(solution)/shard_map/ppermute | solution.py:24
  173.6 5.6 %fusion.9 = bf16[1,1,512,3584]{3,2,1,0:T(8,128)(2,1)} fusion(bf16[768,512]{1,0:T(8,128)(2,1)S(1)} %bitcast.353, bf16[192,3584]{1,0:T(8,128)(2,1)S(1)} %copy-done.27, bf16[192,3584]{1,0:T(8,128)(2,1)} %collective-permute-done.15.refs_0_, bf16[192,3584]{1,0:T(8,128)(2,1)S(1)} %copy-done.24, bf16[192,3584]{1,0:T(8,128)(2,1)S(1)} %bitcast.313), kind=kOutput, calls=%fused_computation.12 | convolution fusion | flops 2842427392 | bytes 9961472 | tf_op jit(solution)/shard_map/dot_general | solution.py:80
  181.4 24.3 %collective-permute-done.22 = bf16[48,3584]{1,0:T(8,128)(2,1)S(1)} collective-permute-done((bf16[48,3584]{1,0:T(8,128)(2,1)S(1)}, bf16[48,3584]{1,0:T(8,128)(2,1)S(1)}, u32[]{:S(2)}, u32[]{:S(2)}) %collective-permute-start.22) | collective-permute-done | bytes 344096 | tf_op jit(solution)/shard_map/ppermute | solution.py:24
  209.5 2.9 %collective-permute-start.28 = (bf16[2,2,24,3584]{3,2,0,1:T(8,128)(2,1)S(1)}, bf16[2,2,24,3584]{3,2,0,1:T(8,128)(2,1)S(1)}, u32[]{:S(2)}, u32[]{:S(2)}) collective-permute-start(bf16[2,2,24,3584]{3,2,0,1:T(8,128)(2,1)S(1)} %pad_maximum_fusion.7), channel_id=1, source_target_pairs={{0,24},{2,26},{4,28},{6,30},{1,25},{3,27},{5,29},{7,31},{8,0},{10,... | collective-permute-start | bytes 2064392 | tf_op jit(solution)/shard_map/ppermute | solution.py:24
  214.1 2.8 collective-permute-done.25
  222.8 4.9 %collective-permute-done.29 = bf16[2,2,24,3584]{3,2,1,0:T(8,128)(2,1)S(1)} collective-permute-done((bf16[2,2,24,3584]{3,2,1,0:T(8,128)(2,1)S(1)}, bf16[2,2,24,3584]{3,2,1,0:T(8,128)(2,1)S(1)}, u32[]{:S(2)}, u32[]{:S(2)}) %collective-permute-start.29) | collective-permute-done | bytes 688160 | tf_op jit(solution)/shard_map/ppermute | solution.py:24
  227.7 4.5 %collective-permute-done.26 = bf16[64,3584]{1,0:T(8,128)(2,1)S(1)} collective-permute-done((bf16[64,3584]{1,0:T(8,128)(2,1)S(1)}, bf16[64,3584]{1,0:T(8,128)(2,1)S(1)}, u32[]{:S(2)}, u32[]{:S(2)}) %collective-permute-start.26) | collective-permute-done | bytes 458784 | tf_op jit(solution)/shard_map/ppermute | solution.py:24
  240.5 4.6 %fusion.7 = bf16[1,1,3584,512]{3,2,1,0:T(8,128)(2,1)} fusion(bf16[768,3584]{1,0:T(8,128)(2,1)S(1)} %constant_dynamic-update-slice_fusion.85, bf16[768,512]{1,0:T(8,128)(2,1)S(1)} %constant_dynamic-update-slice_fusion.89), kind=kOutput, calls=%fused_computation.10 | convolution fusion | flops 2820407296 | bytes 9961472 | tf_op jit(solution)/shard_map/dot_general | solution.py:80
  245.1 5.5 %collective-permute-done.30 = bf16[2,2,24,3584]{3,2,1,0:T(8,128)(2,1)S(1)} collective-permute-done((bf16[2,2,24,3584]{3,2,1,0:T(8,128)(2,1)S(1)}, bf16[2,2,24,3584]{3,2,1,0:T(8,128)(2,1)S(1)}, u32[]{:S(2)}, u32[]{:S(2)}) %collective-permute-start.30) | collective-permute-done | bytes 688160 | tf_op jit(solution)/shard_map/ppermute | solution.py:24
  251.0 4.5 %collective-permute-done.34 = bf16[128,3584]{1,0:T(8,128)(2,1)S(1)} collective-permute-done((bf16[128,3584]{1,0:T(8,128)(2,1)S(1)}, bf16[128,3584]{1,0:T(8,128)(2,1)S(1)}, u32[]{:S(2)}, u32[]{:S(2)}) %collective-permute-start.34) | collective-permute-done | bytes 917536 | tf_op jit(solution)/shard_map/ppermute | solution.py:24
  256.2 3.0 %collective-permute-start.36 = (bf16[128,3584]{1,0:T(8,128)(2,1)S(1)}, bf16[128,3584]{1,0:T(8,128)(2,1)S(1)}, u32[]{:S(2)}, u32[]{:S(2)}) collective-permute-start(bf16[128,3584]{1,0:T(8,128)(2,1)S(1)} %fusion.18), channel_id=1, source_target_pairs={{32,0},{64,32},{96,64},{33,1},{65,33},{97,65},{34,2},{66,34},{98,6... | collective-permute-start | bytes 2752520 | tf_op jit(solution)/shard_map/ppermute | solution.py:46
  262.2 4.6 %fusion.8 = bf16[1,1,3584,512]{3,2,1,0:T(8,128)(2,1)} fusion(bf16[768,3584]{1,0:T(8,128)(2,1)S(1)} %constant_dynamic-update-slice_fusion.85, bf16[768,512]{1,0:T(8,128)(2,1)S(1)} %constant_dynamic-update-slice_fusion.105), kind=kOutput, calls=%fused_computation.11 | convolution fusion | flops 2820407296 | bytes 9961472 | tf_op jit(solution)/shard_map/dot_general | solution.py:80
  266.7 10.0 %collective-permute-done.36 = bf16[128,3584]{1,0:T(8,128)(2,1)S(1)} collective-permute-done((bf16[128,3584]{1,0:T(8,128)(2,1)S(1)}, bf16[128,3584]{1,0:T(8,128)(2,1)S(1)}, u32[]{:S(2)}, u32[]{:S(2)}) %collective-permute-start.36) | collective-permute-done | bytes 917536 | tf_op jit(solution)/shard_map/ppermute | solution.py:46
  276.7 6.1 %collective-permute-done.33 = bf16[128,3584]{1,0:T(8,128)(2,1)S(1)} collective-permute-done((bf16[128,3584]{1,0:T(8,128)(2,1)S(1)}, bf16[128,3584]{1,0:T(8,128)(2,1)S(1)}, u32[]{:S(2)}, u32[]{:S(2)}) %collective-permute-start.33) | collective-permute-done | bytes 917536 | tf_op jit(solution)/shard_map/ppermute | solution.py:46
  (393 shorter events, 87.7 us)
Async XLA Ops:
  5.8 26.7 %collective-permute-start.1 = (bf16[136,3584]{1,0:T(8,128)(2,1)}, bf16[136,3584]{1,0:T(8,128)(2,1)}, u32[]{:S(2)}, u32[]{:S(2)}) collective-permute-start(bf16[136,3584]{1,0:T(8,128)(2,1)} %fusion.21), channel_id=1, source_target_pairs={{0,4},{2,6},{4,1},{6,3},{1,5},{3,7},{5,0},{7,2},{8,12},{10,14},{12... | collective-permute-start | bytes 2924552 | tf_op jit(solution)/shard_map/ppermute | solution.py:24
  7.7 24.7 %collective-permute-start.2 = (bf16[136,3584]{1,0:T(8,128)(2,1)}, bf16[136,3584]{1,0:T(8,128)(2,1)}, u32[]{:S(2)}, u32[]{:S(2)}) collective-permute-start(bf16[136,3584]{1,0:T(8,128)(2,1)} %fusion.21), channel_id=1, source_target_pairs={{0,5},{2,7},{4,0},{6,2},{1,4},{3,6},{5,1},{7,3},{8,13},{10,15},{12... | collective-permute-start | bytes 2924552 | tf_op jit(solution)/shard_map/ppermute | solution.py:24
  12.5 19.9 %collective-permute-start.3 = (bf16[96,3584]{1,0:T(8,128)(2,1)S(1)}, bf16[96,3584]{1,0:T(8,128)(2,1)S(1)}, u32[]{:S(2)}, u32[]{:S(2)}) collective-permute-start(bf16[96,3584]{1,0:T(8,128)(2,1)S(1)} %pad_maximum_fusion.4), channel_id=1, source_target_pairs={{0,8},{2,10},{4,12},{6,14},{1,9},{3,11},{5,13},{7,15},{8,16},{10,1... | collective-permute-start | bytes 2064392 | tf_op jit(solution)/shard_map/ppermute | solution.py:24
  14.2 18.2 %collective-permute-start.4 = (bf16[96,3584]{1,0:T(8,128)(2,1)S(1)}, bf16[96,3584]{1,0:T(8,128)(2,1)S(1)}, u32[]{:S(2)}, u32[]{:S(2)}) collective-permute-start(bf16[96,3584]{1,0:T(8,128)(2,1)S(1)} %pad_maximum_fusion.5), channel_id=1, source_target_pairs={{0,24},{2,26},{4,28},{6,30},{1,25},{3,27},{5,29},{7,31},{8,0},{10,... | collective-permute-start | bytes 2064392 | tf_op jit(solution)/shard_map/ppermute | solution.py:24
  34.2 13.9 %collective-permute-start.6 = (bf16[72,3584]{1,0:T(8,128)(2,1)S(1)}, bf16[72,3584]{1,0:T(8,128)(2,1)S(1)}, u32[]{:S(2)}, u32[]{:S(2)}) collective-permute-start(bf16[72,3584]{1,0:T(8,128)(2,1)S(1)} %slice.821), channel_id=1, source_target_pairs={{0,5},{2,7},{4,0},{6,2},{1,4},{3,6},{5,1},{7,3},{8,13},{10,15},{12... | collective-permute-start | bytes 1548296 | tf_op jit(solution)/shard_map/ppermute | solution.py:24
  39.6 13.1 %collective-permute-start.5 = (bf16[64,3584]{1,0:T(8,128)(2,1)S(1)}, bf16[64,3584]{1,0:T(8,128)(2,1)S(1)}, u32[]{:S(2)}, u32[]{:S(2)}) collective-permute-start(bf16[64,3584]{1,0:T(8,128)(2,1)S(1)} %slice.820), channel_id=1, source_target_pairs={{0,4},{2,6},{4,1},{6,3},{1,5},{3,7},{5,0},{7,2},{8,12},{10,14},{12... | collective-permute-start | bytes 1376264 | tf_op jit(solution)/shard_map/ppermute | solution.py:24
  39.6 18.6 %collective-permute-start.7 = (bf16[96,3584]{1,0:T(8,128)(2,1)S(1)}, bf16[96,3584]{1,0:T(8,128)(2,1)S(1)}, u32[]{:S(2)}, u32[]{:S(2)}) collective-permute-start(bf16[96,3584]{1,0:T(8,128)(2,1)S(1)} %pad_maximum_fusion.6), channel_id=1, source_target_pairs={{0,16},{2,18},{4,20},{6,22},{1,17},{3,19},{5,21},{7,23},{8,24},{10... | collective-permute-start | bytes 2064392 | tf_op jit(solution)/shard_map/ppermute | solution.py:24
  58.5 31.9 %collective-permute-start.8 = (bf16[192,3584]{1,0:T(8,128)(2,1)S(1)}, bf16[192,3584]{1,0:T(8,128)(2,1)S(1)}, u32[]{:S(2)}, u32[]{:S(2)}) collective-permute-start(bf16[192,3584]{1,0:T(8,128)(2,1)S(1)} %get-tuple-element.360), channel_id=1, source_target_pairs={{0,4},{2,6},{4,1},{6,3},{1,5},{3,7},{5,0},{7,2},{8,12},{10,14},{12... | collective-permute-start | bytes 4128776 | tf_op jit(solution)/shard_map/ppermute | solution.py:24
  58.5 31.8 %collective-permute-start.9 = (bf16[192,3584]{1,0:T(8,128)(2,1)S(1)}, bf16[192,3584]{1,0:T(8,128)(2,1)S(1)}, u32[]{:S(2)}, u32[]{:S(2)}) collective-permute-start(bf16[192,3584]{1,0:T(8,128)(2,1)S(1)} %get-tuple-element.360), channel_id=1, source_target_pairs={{0,5},{2,7},{4,0},{6,2},{1,4},{3,6},{5,1},{7,3},{8,13},{10,15},{12... | collective-permute-start | bytes 4128776 | tf_op jit(solution)/shard_map/ppermute | solution.py:24
  65.2 33.7 %collective-permute-start.11 = (bf16[192,3584]{1,0:T(8,128)(2,1)S(1)}, bf16[192,3584]{1,0:T(8,128)(2,1)S(1)}, u32[]{:S(2)}, u32[]{:S(2)}) collective-permute-start(bf16[192,3584]{1,0:T(8,128)(2,1)S(1)} %bitcast.356), channel_id=1, source_target_pairs={{0,8},{2,10},{4,12},{6,14},{1,9},{3,11},{5,13},{7,15},{8,16},{10,1... | collective-permute-start | bytes 4128776 | tf_op jit(solution)/shard_map/ppermute | solution.py:24
  66.9 32.1 %collective-permute-start.12 = (bf16[192,3584]{1,0:T(8,128)(2,1)S(1)}, bf16[192,3584]{1,0:T(8,128)(2,1)S(1)}, u32[]{:S(2)}, u32[]{:S(2)}) collective-permute-start(bf16[192,3584]{1,0:T(8,128)(2,1)S(1)} %bitcast.355), channel_id=1, source_target_pairs={{0,24},{2,26},{4,28},{6,30},{1,25},{3,27},{5,29},{7,31},{8,0},{10,... | collective-permute-start | bytes 4128776 | tf_op jit(solution)/shard_map/ppermute | solution.py:24
  100.2 33.2 %collective-permute-start.14 = (bf16[192,3584]{1,0:T(8,128)(2,1)S(1)}, bf16[192,3584]{1,0:T(8,128)(2,1)}, u32[]{:S(2)}, u32[]{:S(2)}) collective-permute-start(bf16[192,3584]{1,0:T(8,128)(2,1)S(1)} %get-tuple-element.218.refs_2_), channel_id=1, source_target_pairs={{0,1},{2,3},{4,5},{6,7},{1,0},{3,2},{5,4},{7,6},{8,9},{10,11},{12,... | collective-permute-start | bytes 4128776 | tf_op jit(solution)/shard_map/ppermute | solution.py:24
  101.0 33.2 %collective-permute-start.15 = (bf16[192,3584]{1,0:T(8,128)(2,1)}, bf16[192,3584]{1,0:T(8,128)(2,1)}, u32[]{:S(2)}, u32[]{:S(2)}) collective-permute-start(bf16[192,3584]{1,0:T(8,128)(2,1)} %bitcast.61), channel_id=1, source_target_pairs={{0,16},{2,18},{4,20},{6,22},{1,17},{3,19},{5,21},{7,23},{8,24},{10... | collective-permute-start | bytes 4128776 | tf_op jit(solution)/shard_map/ppermute | solution.py:24
  134.1 30.7 %collective-permute-start.16 = (bf16[192,3584]{1,0:T(8,128)(2,1)}, bf16[192,3584]{1,0:T(8,128)(2,1)}, u32[]{:S(2)}, u32[]{:S(2)}) collective-permute-start(bf16[192,3584]{1,0:T(8,128)(2,1)} %get-tuple-element.177), channel_id=1, source_target_pairs={{0,5},{2,7},{4,0},{6,2},{1,4},{3,6},{5,1},{7,3},{8,13},{10,15},{12... | collective-permute-start | bytes 4128776 | tf_op jit(solution)/shard_map/ppermute | solution.py:24
  135.0 31.8 %collective-permute-start.17 = (bf16[192,3584]{1,0:T(8,128)(2,1)}, bf16[192,3584]{1,0:T(8,128)(2,1)}, u32[]{:S(2)}, u32[]{:S(2)}) collective-permute-start(bf16[192,3584]{1,0:T(8,128)(2,1)} %get-tuple-element.178), channel_id=1, source_target_pairs={{0,4},{2,6},{4,1},{6,3},{1,5},{3,7},{5,0},{7,2},{8,12},{10,14},{12... | collective-permute-start | bytes 4128776 | tf_op jit(solution)/shard_map/ppermute | solution.py:24
  136.2 22.9 %collective-permute-start.18 = (bf16[144,3584]{1,0:T(8,128)(2,1)}, bf16[144,3584]{1,0:T(8,128)(2,1)}, u32[]{:S(2)}, u32[]{:S(2)}) collective-permute-start(bf16[144,3584]{1,0:T(8,128)(2,1)} %get-tuple-element.179), channel_id=1, source_target_pairs={{0,24},{2,26},{4,28},{6,30},{1,25},{3,27},{5,29},{7,31},{8,0},{10,... | collective-permute-start | bytes 3096584 | tf_op jit(solution)/shard_map/ppermute | solution.py:24
  138.9 23.5 %collective-permute-start.19 = (bf16[144,3584]{1,0:T(8,128)(2,1)}, bf16[144,3584]{1,0:T(8,128)(2,1)}, u32[]{:S(2)}, u32[]{:S(2)}) collective-permute-start(bf16[144,3584]{1,0:T(8,128)(2,1)} %get-tuple-element.180), channel_id=1, source_target_pairs={{0,8},{2,10},{4,12},{6,14},{1,9},{3,11},{5,13},{7,15},{8,16},{10,1... | collective-permute-start | bytes 3096584 | tf_op jit(solution)/shard_map/ppermute | solution.py:24
  166.9 39.2 %collective-permute-start.20 = (bf16[192,3584]{1,0:T(8,128)(2,1)S(1)}, bf16[192,3584]{1,0:T(8,128)(2,1)S(1)}, u32[]{:S(2)}, u32[]{:S(2)}) collective-permute-start(bf16[192,3584]{1,0:T(8,128)(2,1)S(1)} %get-tuple-element.196), channel_id=1, source_target_pairs={{0,1},{2,3},{4,5},{6,7},{1,0},{3,2},{5,4},{7,6},{8,9},{10,11},{12,... | collective-permute-start | bytes 4128776 | tf_op jit(solution)/shard_map/ppermute | solution.py:24
  168.3 37.8 %collective-permute-start.21 = (bf16[192,3584]{1,0:T(8,128)(2,1)S(1)}, bf16[192,3584]{1,0:T(8,128)(2,1)S(1)}, u32[]{:S(2)}, u32[]{:S(2)}) collective-permute-start(bf16[192,3584]{1,0:T(8,128)(2,1)S(1)} %get-tuple-element.198), channel_id=1, source_target_pairs={{0,16},{2,18},{4,20},{6,22},{1,17},{3,19},{5,21},{7,23},{8,24},{10... | collective-permute-start | bytes 4128776 | tf_op jit(solution)/shard_map/ppermute | solution.py:24
  170.4 35.7 %collective-permute-start.24 = (bf16[96,3584]{1,0:T(8,128)(2,1)S(1)}, bf16[96,3584]{1,0:T(8,128)(2,1)S(1)}, u32[]{:S(2)}, u32[]{:S(2)}) collective-permute-start(bf16[96,3584]{1,0:T(8,128)(2,1)S(1)} %slice.905), channel_id=1, source_target_pairs={{0,2},{2,0},{4,6},{6,4},{1,3},{3,1},{5,7},{7,5},{8,10},{10,8},{12,... | collective-permute-start | bytes 2064392 | tf_op jit(solution)/shard_map/ppermute | solution.py:24
  170.4 35.4 %collective-permute-start.22 = (bf16[48,3584]{1,0:T(8,128)(2,1)S(1)}, bf16[48,3584]{1,0:T(8,128)(2,1)S(1)}, u32[]{:S(2)}, u32[]{:S(2)}) collective-permute-start(bf16[48,3584]{1,0:T(8,128)(2,1)S(1)} %get-tuple-element.199), channel_id=1, source_target_pairs={{0,24},{2,26},{4,28},{6,30},{1,25},{3,27},{5,29},{7,31},{8,0},{10,... | collective-permute-start | bytes 1032200 | tf_op jit(solution)/shard_map/ppermute | solution.py:24
  171.7 34.4 %collective-permute-start.23 = (bf16[48,3584]{1,0:T(8,128)(2,1)S(1)}, bf16[48,3584]{1,0:T(8,128)(2,1)S(1)}, u32[]{:S(2)}, u32[]{:S(2)}) collective-permute-start(bf16[48,3584]{1,0:T(8,128)(2,1)S(1)} %get-tuple-element.200), channel_id=1, source_target_pairs={{0,8},{2,10},{4,12},{6,14},{1,9},{3,11},{5,13},{7,15},{8,16},{10,1... | collective-permute-start | bytes 1032200 | tf_op jit(solution)/shard_map/ppermute | solution.py:24
  209.0 18.7 %collective-permute-start.29 = (bf16[2,2,24,3584]{3,2,1,0:T(8,128)(2,1)S(1)}, bf16[2,2,24,3584]{3,2,1,0:T(8,128)(2,1)S(1)}, u32[]{:S(2)}, u32[]{:S(2)}) collective-permute-start(bf16[2,2,24,3584]{3,2,1,0:T(8,128)(2,1)S(1)} %pad_maximum_fusion.8), channel_id=1, source_target_pairs={{0,8},{2,10},{4,12},{6,14},{1,9},{3,11},{5,13},{7,15},{8,16},{10,1... | collective-permute-start | bytes 2064392 | tf_op jit(solution)/shard_map/ppermute | solution.py:24
  209.5 18.2 %collective-permute-start.28 = (bf16[2,2,24,3584]{3,2,0,1:T(8,128)(2,1)S(1)}, bf16[2,2,24,3584]{3,2,0,1:T(8,128)(2,1)S(1)}, u32[]{:S(2)}, u32[]{:S(2)}) collective-permute-start(bf16[2,2,24,3584]{3,2,0,1:T(8,128)(2,1)S(1)} %pad_maximum_fusion.7), channel_id=1, source_target_pairs={{0,24},{2,26},{4,28},{6,30},{1,25},{3,27},{5,29},{7,31},{8,0},{10,... | collective-permute-start | bytes 2064392 | tf_op jit(solution)/shard_map/ppermute | solution.py:24
  218.3 13.9 %collective-permute-start.26 = (bf16[64,3584]{1,0:T(8,128)(2,1)S(1)}, bf16[64,3584]{1,0:T(8,128)(2,1)S(1)}, u32[]{:S(2)}, u32[]{:S(2)}) collective-permute-start(bf16[64,3584]{1,0:T(8,128)(2,1)S(1)} %get-tuple-element.354), channel_id=1, source_target_pairs={{0,4},{2,6},{4,1},{6,3},{1,5},{3,7},{5,0},{7,2},{8,12},{10,14},{12... | collective-permute-start | bytes 1376264 | tf_op jit(solution)/shard_map/ppermute | solution.py:24
  219.0 13.1 %collective-permute-start.27 = (bf16[64,3584]{1,0:T(8,128)(2,1)S(1)}, bf16[64,3584]{1,0:T(8,128)(2,1)S(1)}, u32[]{:S(2)}, u32[]{:S(2)}) collective-permute-start(bf16[64,3584]{1,0:T(8,128)(2,1)S(1)} %get-tuple-element.353), channel_id=1, source_target_pairs={{0,5},{2,7},{4,0},{6,2},{1,4},{3,6},{5,1},{7,3},{8,13},{10,15},{12... | collective-permute-start | bytes 1376264 | tf_op jit(solution)/shard_map/ppermute | solution.py:24
  232.3 18.2 %collective-permute-start.30 = (bf16[2,2,24,3584]{3,2,1,0:T(8,128)(2,1)S(1)}, bf16[2,2,24,3584]{3,2,1,0:T(8,128)(2,1)S(1)}, u32[]{:S(2)}, u32[]{:S(2)}) collective-permute-start(bf16[2,2,24,3584]{3,2,1,0:T(8,128)(2,1)S(1)} %pad_maximum_fusion.9), channel_id=1, source_target_pairs={{0,16},{2,18},{4,20},{6,22},{1,17},{3,19},{5,21},{7,23},{8,24},{10... | collective-permute-start | bytes 2064392 | tf_op jit(solution)/shard_map/ppermute | solution.py:24
  233.0 22.5 %collective-permute-start.34 = (bf16[128,3584]{1,0:T(8,128)(2,1)S(1)}, bf16[128,3584]{1,0:T(8,128)(2,1)S(1)}, u32[]{:S(2)}, u32[]{:S(2)}) collective-permute-start(bf16[128,3584]{1,0:T(8,128)(2,1)S(1)} %pad_maximum_fusion.1), channel_id=1, source_target_pairs={{0,4},{2,6},{4,1},{6,3},{1,5},{3,7},{5,0},{7,2},{8,12},{10,14},{12... | collective-permute-start | bytes 2752520 | tf_op jit(solution)/shard_map/ppermute | solution.py:24
  234.0 21.5 %collective-permute-start.35 = (bf16[128,3584]{1,0:T(8,128)(2,1)S(1)}, bf16[128,3584]{1,0:T(8,128)(2,1)S(1)}, u32[]{:S(2)}, u32[]{:S(2)}) collective-permute-start(bf16[128,3584]{1,0:T(8,128)(2,1)S(1)} %pad_maximum_fusion.2), channel_id=1, source_target_pairs={{0,5},{2,7},{4,0},{6,2},{1,4},{3,6},{5,1},{7,3},{8,13},{10,15},{12... | collective-permute-start | bytes 2752520 | tf_op jit(solution)/shard_map/ppermute | solution.py:24
  236.7 22.5 %collective-permute-start.31 = (bf16[3,2,24,3584]{3,2,1,0:T(8,128)(2,1)S(1)}, bf16[3,2,24,3584]{3,2,1,0:T(8,128)(2,1)S(1)}, u32[]{:S(2)}, u32[]{:S(2)}) collective-permute-start(bf16[3,2,24,3584]{3,2,1,0:T(8,128)(2,1)S(1)} %pad_maximum_fusion), channel_id=1, source_target_pairs={{0,2},{2,0},{4,6},{6,4},{1,3},{3,1},{5,7},{7,5},{8,10},{10,8},{12,... | collective-permute-start | bytes 3096584 | tf_op jit(solution)/shard_map/ppermute | solution.py:24
  256.2 20.6 %collective-permute-start.36 = (bf16[128,3584]{1,0:T(8,128)(2,1)S(1)}, bf16[128,3584]{1,0:T(8,128)(2,1)S(1)}, u32[]{:S(2)}, u32[]{:S(2)}) collective-permute-start(bf16[128,3584]{1,0:T(8,128)(2,1)S(1)} %fusion.18), channel_id=1, source_target_pairs={{32,0},{64,32},{96,64},{33,1},{65,33},{97,65},{34,2},{66,34},{98,6... | collective-permute-start | bytes 2752520 | tf_op jit(solution)/shard_map/ppermute | solution.py:46
  260.8 22.0 %collective-permute-start.33 = (bf16[128,3584]{1,0:T(8,128)(2,1)S(1)}, bf16[128,3584]{1,0:T(8,128)(2,1)S(1)}, u32[]{:S(2)}, u32[]{:S(2)}) collective-permute-start(bf16[128,3584]{1,0:T(8,128)(2,1)S(1)} %fusion.19), channel_id=1, source_target_pairs={{0,32},{32,64},{64,96},{1,33},{33,65},{65,97},{2,34},{34,66},{66,9... | collective-permute-start | bytes 2752520 | tf_op jit(solution)/shard_map/ppermute | solution.py:46
  (81 other events, 641.0 us)
